TPU v7x, 256 devices: a whole 4x4x8 slice. The times are simulated.
256 devices in a mesh: dp: 32 (over z_hi, x, core), node: 8 (over y, z_lo).
Axes of the slice: x: 4, y: 4, z: 8 (z_hi: 4, z_lo: 2; z = z_hi * 2 + z_lo), core: 2. Of those that a mesh axis runs over, the one named last changes fastest.
Arguments:
- x_band: bfloat16 [32768, 512], P(('dp', 'node')), may hold values from -6 to 6
- d_gate_up: bfloat16 [32768, 18432], P(('dp', 'node')), may hold values from -0.125 to 0.125
- owner: int32 [36], replicated, may hold values from 0 to 31, as said below
- stat_left: float32 [32, 2, 512, 512], P('dp', None, 'node'), as said below
- stat_right: float32 [32, 2, 512, 512], P('dp', None, 'node'), as said below
Outputs:
- directions: bfloat16 [512, 18432], P('node')
- stat_left_new: float32 [32, 2, 512, 512], P('dp', None, 'node')
- stat_right_new: float32 [32, 2, 512, 512], P('dp', None, 'node')
Inputs may be any that keep to these rules, and one draw needn't show every extreme that they name: owner[0], ..., owner[31] name every index of dp once, and owner[b] = owner[b - 32] for b >= 32; block b sits in slot b // 32 of its owner. Each stat_left[o, s] is symmetric positive definite. Each stat_right[o, s] is symmetric positive definite.
All inputs are finite; a program needn't handle non-finite values.
Results may differ from a plain program's by a relative error of at most 0.023.
Values may be sent and summed in bfloat16 or wider, within the bound.
No kernel may reach another device: no remote copies, remote signals or barrier semaphores. Data moves between devices by JAX's collectives and lax.ppermute only.
A program may use at most 128 MiB of HBM per device.

v0:
```python
import jax
import jax.numpy as jnp
from jax import lax
from jax.sharding import PartitionSpec as P

B = 512
SLOTS = 2
ITERS = 2


BETA = 0.9


def batched(first_matrix, second_matrix):
    return jnp.einsum("kij,kjl->kil", first_matrix, second_matrix, precision=lax.Precision.HIGHEST)


def newton_root(statistic):
    block_order = statistic.shape[-1]
    identity = jnp.eye(block_order, dtype=statistic.dtype)
    norm_scale = block_order * jnp.sqrt(jnp.mean(statistic * statistic, axis=(1, 2)) + 1e-06)
    inverse_root = identity[None] * (norm_scale ** (-0.25))[:, None, None]
    moment = statistic / norm_scale[:, None, None]
    for iteration in range(ITERS):
        factor = (5.0 * identity - moment) * 0.25
        inverse_root = batched(inverse_root, factor)
        if iteration + 1 < ITERS:
            square = batched(factor, factor)
            fourth = batched(square, square)
            moment = batched(fourth, moment)
    return inverse_root


def contract(columns, stacked):
    return jnp.einsum("tr,tkc->krc", columns, stacked, preferred_element_type=jnp.float32)


def shards(x_band, d_gate_up, owner, stat_left, stat_right):
    dp_count = lax.axis_size("dp")
    node_count = lax.axis_size("node")
    my_owner = lax.axis_index("dp")
    my_node = lax.axis_index("node")
    tokens_here = x_band.shape[0]
    bucket = d_gate_up.shape[1] // B
    extra_count = bucket - dp_count
    piece_rows = B // node_count
    cotangent = d_gate_up.reshape(tokens_here, bucket, B)
    first_owners = owner[:dp_count]
    owner_ids = jnp.arange(dp_count, dtype=jnp.int32)
    position = jnp.sum(
        owner_ids[None, :] * (first_owners[None, :] == owner_ids[:, None]).astype(jnp.int32), axis=1
    )
    mine_first = position[my_owner]
    has_extra = (mine_first < extra_count).astype(jnp.float32)
    chosen_extra = jnp.minimum(mine_first, extra_count - 1)
    ordered = jnp.take(cotangent, position, axis=1)
    own_block = lax.psum_scatter(
        contract(x_band, ordered).reshape(B * lax.axis_size("dp"), B).astype(jnp.bfloat16),
        "dp",
        scatter_dimension=0,
        tiled=True,
    ).astype(jnp.float32)
    extra_term = contract(x_band, cotangent[:, dp_count:, :])
    extra_sum = lax.psum(extra_term.astype(jnp.bfloat16), "dp").astype(jnp.float32)
    extra_block = lax.dynamic_index_in_dim(extra_sum, chosen_extra, 0, keepdims=False) * has_extra
    grad_rows = lax.psum_scatter(
        jnp.stack([own_block, extra_block]).astype(jnp.bfloat16),
        "node",
        scatter_dimension=1,
        tiled=True,
    )
    grad_full = lax.all_gather(grad_rows, "node", axis=1, tiled=True)
    column_piece = lax.dynamic_slice_in_dim(grad_full, my_node * piece_rows, piece_rows, 2)
    left_rows = (
        BETA * stat_left[0]
        + jnp.einsum("sic,sjc->sij", grad_rows, grad_full, preferred_element_type=jnp.float32) / B
    )
    right_rows = (
        BETA * stat_right[0]
        + jnp.einsum("sci,scj->sij", column_piece, grad_full, preferred_element_type=jnp.float32)
        / B
    )
    problem_count = 2 * SLOTS
    left_full, right_full = (
        lax.all_gather(left_rows.astype(jnp.bfloat16), "node", axis=1, tiled=True).astype(
            left_rows.dtype
        ),
        lax.all_gather(right_rows.astype(jnp.bfloat16), "node", axis=1, tiled=True).astype(
            right_rows.dtype
        ),
    )
    problems = jnp.stack([left_full, right_full], axis=1).reshape(problem_count, B, B)
    inverse_roots = newton_root(problems).astype(jnp.bfloat16)
    inverse_roots = inverse_roots.reshape(SLOTS, 2, B, B)
    left_root = inverse_roots[:, 0]
    right_root = inverse_roots[:, 1]
    root_rows = lax.dynamic_slice_in_dim(left_root, my_node * piece_rows, piece_rows, 1)
    half_product = jnp.einsum(
        "sij,sjc->sic", root_rows, grad_full, preferred_element_type=jnp.float32
    ).astype(jnp.bfloat16)
    direction_rows = jnp.einsum(
        "sic,scd->isd", half_product, right_root, preferred_element_type=jnp.float32
    ).astype(jnp.bfloat16)
    everyone = lax.all_gather(direction_rows, "dp", axis=1, tiled=True)
    take_index = owner * SLOTS + jnp.arange(bucket, dtype=jnp.int32) // dp_count
    picked = jnp.take(everyone, take_index, axis=1)
    directions = picked.reshape(piece_rows, bucket * B)
    return (directions, left_rows[None], right_rows[None])


def solution(mesh):
    placed = (
        P(("dp", "node"), None),
        P(("dp", "node"), None),
        P(),
        P("dp", None, "node", None),
        P("dp", None, "node", None),
    )
    return jax.shard_map(
        shards,
        mesh=mesh,
        in_specs=placed,
        out_specs=(P("node", None), P("dp", None, "node", None), P("dp", None, "node", None)),
        check_vma=False,
    )
```

profile of v0, /device:TPU:1, one launch (start us, length us, event | category | flops | bytes accessed | tf_op | source)
XLA Modules:
  0.0 825.9 jit_solution(13439883342216507763)
XLA Ops:
  7.2 6.6 copy.40
  13.9 3.1 convert_bitcast_fusion
  16.9 0.0 reduce-scatter.2.cloned.1.call-start
  17.0 0.1 select_reduce_fusion
  17.1 5.4 gather_fusion
  22.6 10.4 %convolution_convert_fusion = bf16[32,512,512]{1,2,0:T(8,128)(2,1)} fusion(bf16[32,128,512]{1,2,0:T(8,128)(2,1)} %gather_fusion, pred[32]{0:T(512)(128)(4,1)S(1)} %compare_and_fusion, bf16[128,512]{1,0:T(8,128)(2,1)S(1)} %copy-done), kind=kOutput, calls=%fused_computation.2 | convolution fusion | flops 2157969408 | bytes 21102624 | tf_op jit(solution)/shard_map/tr,tkc->krc/dot_general | solution.py:35
  33.0 21.3 %copy.43 = bf16[16384,512]{0,1:T(8,128)(2,1)} copy(bf16[16384,512]{1,0:T(8,128)(2,1)} %bitcast.55) | data formatting | bytes 33554432 | tf_op jit(solution)/shard_map/convert_element_type | solution.py:58
  54.4 0.0 all-reduce.6.cloned.1.call-start
  54.4 0.6 dynamic_slice.15
  56.3 255.8 %all-reduce.4.cloned.1.call-done = bf16[4,512,512]{1,2,0:T(8,128)(2,1)} async-done(((bf16[4,512,512]{1,2,0:T(8,128)(2,1)}), bf16[4,512,512]{1,2,0:T(8,128)(2,1)}) %all-reduce.4.cloned.1.call-update) | async-done | bytes 2097168 | tf_op jit(solution)/shard_map/psum | solution.py:64
  312.1 1.1 multiply_convert_fusion
  313.2 168.9 %reduce-scatter.2.cloned.1.call-done = bf16[512,512]{0,1:T(8,128)(2,1)} async-done(((bf16[16384,512]{0,1:T(8,128)(2,1)}), bf16[512,512]{0,1:T(8,128)(2,1)}) %reduce-scatter.2.cloned.1.call-update) | async-done | bytes 524304 | tf_op jit(solution)/shard_map/reduce_scatter | solution.py:57
  482.1 1.1 pad_maximum_fusion
  483.2 2.1 copy.44
  485.4 0.0 all-gather.5.cloned.1.call-start
  485.4 0.6 dynamic-slice.1
  486.7 78.7 %all-reduce.6.cloned.1.call-done = bf16[2,512,512]{2,0,1:T(2,128)(2,1)} async-done(((bf16[2,512,512]{2,0,1:T(2,128)(2,1)}), bf16[2,512,512]{2,0,1:T(2,128)(2,1)}) %all-reduce.6.cloned.1.call-update) | async-done | bytes 1048592
  565.3 1.6 constant_dynamic-slice_fusion.1
  567.0 0.0 all-gather.7.cloned.1.call-start
  567.0 42.6 %all-gather.5.cloned.1.call-done = bf16[2,512,512]{2,0,1:T(2,128)(2,1)} async-done(((bf16[2,64,512]{2,0,1:T(2,128)(2,1)}), bf16[2,512,512]{2,0,1:T(2,128)(2,1)}) %all-gather.5.cloned.1.call-update) | async-done | bytes 1048592 | tf_op jit(solution)/shard_map/all_gather | solution.py:72
  609.6 2.5 fusion.47
  612.2 0.0 all-gather.9.cloned.1.call-start
  612.2 1.3 constant_dynamic-slice_fusion
  613.5 2.3 fusion.46
  615.9 0.5 all-gather.11.cloned.1.call-start
  616.4 0.1 fusion.24
  616.5 0.1 fusion.25
  616.6 37.7 %all-gather.7.cloned.1.call-done = bf16[2,512,512]{2,1,0:T(8,128)(2,1)} async-done(((bf16[2,64,512]{2,1,0:T(8,128)(2,1)}), bf16[2,512,512]{2,1,0:T(8,128)(2,1)}) %all-gather.7.cloned.1.call-update) | async-done | bytes 1048592 | tf_op jit(solution)/shard_map/all_gather | solution.py:85
  654.3 44.4 %all-gather.9.cloned.1.call-done = bf16[2,512,512]{2,1,0:T(8,128)(2,1)} async-done(((bf16[2,64,512]{2,1,0:T(8,128)(2,1)}), bf16[2,512,512]{2,1,0:T(8,128)(2,1)}) %all-gather.9.cloned.1.call-update) | async-done | bytes 1048592 | tf_op jit(solution)/shard_map/all_gather | solution.py:88
  698.7 2.2 multiply_reduce_fusion
  700.8 3.8 maximum_convert_fusion
  704.6 0.1 copy.49
  704.7 0.1 mul.93
  704.8 2.6 copy.50
  707.5 0.6 bitcast_divide_fusion
  708.0 7.7 fusion.8
  715.7 7.3 fusion.48
  723.0 7.3 fusion.49
  730.3 7.9 fusion.5
  738.2 7.4 fusion.18
  745.6 1.3 copy-done.3
  746.9 0.1 slice.20
  747.0 2.4 fusion.23
  749.4 0.1 broadcast_in_dim.40
  749.6 64.3 %all-gather.11.cloned.1.call-done = bf16[64,64,512]{2,0,1:T(8,128)(2,1)} async-done(((bf16[64,2,512]{2,0,1:T(8,128)(2,1)}), bf16[64,64,512]{2,0,1:T(8,128)(2,1)}) %all-gather.11.cloned.1.call-update) | async-done | bytes 4194320 | tf_op jit(solution)/shard_map/all_gather | solution.py:104
  813.9 2.9 gather_fusion.1
  816.8 0.2 copy.59
  817.0 1.8 broadcast_select_fusion
  (31 shorter events, 0.3 us)
Async XLA Ops:
  7.2 6.7 copy-start
  7.2 304.9 %all-reduce.4.cloned.1.call-start = ((), (), s32[]{:S(2)}) async-start(), calls=%async_computation.2 | async-start | bytes 4194304 | tf_op jit(solution)/shard_map/psum | solution.py:64
  13.9 3.1 copy-start.6
  16.9 465.1 %reduce-scatter.2.cloned.1.call-start = ((), (), s32[]{:S(2)}) async-start(), calls=%async_computation.1 | async-start | bytes 17301504 | tf_op jit(solution)/shard_map/reduce_scatter | solution.py:57
  54.3 431.1 %copy-start.7 = (u32[256]{0:T(256)S(1)}, u32[256]{0:T(256)}, u32[]{:S(2)}) copy-start(u32[256]{0:T(256)} %constant.104) | copy-start | bytes 3076
  54.4 555.3 %copy-start.4 = (f32[1,2,64,512]{3,2,1,0:T(8,128)S(1)}, f32[1,2,64,512]{3,2,1,0:T(8,128)}, u32[]{:S(2)}) copy-start(f32[1,2,64,512]{3,2,1,0:T(8,128)} %param.8) | copy-start | bytes 786436
  54.4 510.9 %all-reduce.6.cloned.1.call-start = ((), (), s32[]{:S(2)}) async-start(), calls=%async_computation.7 | async-start | bytes 2097152
  313.2 300.3 %copy-start.5 = (f32[1,2,64,512]{3,2,1,0:T(8,128)S(1)}, f32[1,2,64,512]{3,2,1,0:T(8,128)}, u32[]{:S(2)}) copy-start(f32[1,2,64,512]{3,2,1,0:T(8,128)} %param.9) | copy-start | bytes 786436
  485.4 124.3 %all-gather.5.cloned.1.call-start = ((), (), s32[]{:S(2)}) async-start(), calls=%async_computation.3 | async-start | bytes 1179648 | tf_op jit(solution)/shard_map/all_gather | solution.py:72
  567.0 87.3 %all-gather.7.cloned.1.call-start = ((), (), s32[]{:S(2)}) async-start(), calls=%async_computation.4 | async-start | bytes 1179648 | tf_op jit(solution)/shard_map/all_gather | solution.py:85
  612.2 86.5 %all-gather.9.cloned.1.call-start = ((), (), s32[]{:S(2)}) async-start(), calls=%async_computation.5 | async-start | bytes 1179648 | tf_op jit(solution)/shard_map/all_gather | solution.py:88
  615.9 198.0 %all-gather.11.cloned.1.call-start = ((), (), s32[]{:S(2)}) async-start(), calls=%async_computation.6 | async-start | bytes 4325376 | tf_op jit(solution)/shard_map/all_gather | solution.py:104
  738.2 8.8 %copy-start.2 = (bf16[2,512,512]{2,0,1:T(2,128)(2,1)S(1)}, bf16[2,512,512]{2,0,1:T(2,128)(2,1)}, u32[]{:S(2)}) copy-start(bf16[2,512,512]{2,0,1:T(2,128)(2,1)} %all-gather.5.cloned.1.call-done) | copy-start | bytes 3145732
  745.6 1.3 copy-start.3
  816.8 2.0 copy-start.1
Sparse Core Ops, SparseCore 0:
  17.1 294.9 all-reduce.3
  316.9 165.1 reduce-scatter.1
  485.5 79.7 all-reduce.5
  567.7 41.9 all-gather.4
  612.3 41.9 all-gather.6
  656.7 41.9 all-gather.8
  749.5 64.2 all-gather.10
where the time goes:
time: 832 us; the launch traced here: 826 us
  waiting for transfers between devices  692 us (83%)
  matrix products  58.2 us (7%)
  local copies, waits for them, and re-layouts  47 us (6%)
  between operations  16.5 us (2%)
  other arithmetic  10.9 us (1%)
    psum x1, waiting for transfers between devices, shards(): lax.psum(extra_term.astype(jnp.bfloat16), 'dp').astype(jnp.float32)  256 us
    reduce_scatter x1, waiting for transfers between devices, shards(): lax.psum_scatter(contract(x_band, ordered).reshape(B * lax.axis_size('dp'...  169 us
    unnamed x8, waiting for transfers between devices  78.8 us
    all_gather x1, waiting for transfers between devices, shards(): everyone = lax.all_gather(direction_rows, 'dp', axis=1, tiled=True)  64.3 us
    all_gather x1, waiting for transfers between devices, shards(): lax.all_gather(right_rows.astype(jnp.bfloat16), 'node', axis=1, tiled=True)  44.4 us
    all_gather x1, waiting for transfers between devices, shards(): grad_full = lax.all_gather(grad_rows, 'node', axis=1, tiled=True)  42.6 us
    all_gather x1, waiting for transfers between devices, shards(): lax.all_gather(left_rows.astype(jnp.bfloat16), 'node', axis=1, tiled=True)  37.7 us
    dot_general x5, matrix products, batched(): jnp.einsum('kij,kjl->kil', first_matrix, second_matrix, precision=lax.Pre...  37.6 us
  transfers between devices with their start and end apart: 7, of which 7 were waited for; matrix products, arithmetic and copies ran while one was open for 5% of the time, Pallas kernels for 0%

commit v1 on v0

v1 whole, which is shorter than its diff:
```python
import math

import jax
import jax.numpy as jnp
import numpy as np
from jax import lax
from jax.experimental import pallas as pl
from jax.experimental.pallas import tpu as pltpu
from jax.sharding import Mesh, PartitionSpec as P

B = 512
SLOTS = 2
BETA = 0.9
EXTRA_CHUNK = 128
FLOW = B + EXTRA_CHUNK
HALF = B // 2

FINE = ("z_hi", "x", "core", "y", "z_lo")
FINE_SIZES = (4, 4, 2, 4, 2)
VMEM_LIMIT = 48 * 1024 * 1024

COEF = [6.25 / 4, -(1.25 + 1.25**5) / 4] + [
    -math.comb(5, k) * 1.25 ** (5 - k) * (-0.25) ** k / 4 for k in range(1, 6)
]

ANY = pl.BlockSpec(memory_space=pl.ANY)
SMEM = pl.BlockSpec(memory_space=pltpu.SMEM)
VMEM = pl.BlockSpec(memory_space=pltpu.VMEM)
PARAMS = pltpu.CompilerParams(vmem_limit_bytes=VMEM_LIMIT)


def swap(value, axis, mask):
    size = FINE_SIZES[FINE.index(axis)]
    return lax.ppermute(value, axis, [(i, i ^ mask) for i in range(size)])


def swap_core(value, axis, mask):
    size = FINE_SIZES[FINE.index(axis)]
    if axis == "x":
        pairs = [(i * 2 + c, (i ^ mask) * 2 + 1 - c) for i in range(size) for c in range(2)]
        return lax.ppermute(value, ("x", "core"), pairs)
    pairs = [(c * size + i, (1 - c) * size + (i ^ mask)) for i in range(size) for c in range(2)]
    return lax.ppermute(value, ("core", "y"), pairs)


def aligned(index, step):
    return pl.multiple_of(index * step, step)


def fill_positions(owner, position):
    for block in range(32):
        position[owner[block]] = block


X_MSG = 3 * FLOW + B
Y_MSG = 3 * B + B
OWN_MSG = 2 * FLOW + 2 * B + B
X_FWD = slice(2 * FLOW, 3 * FLOW + HALF)
Y_FWD = slice(2 * B, 3 * B + HALF)


def pack_kernel(owner, place, d, xb, own, core, x1c, x1s, x3c, x3s, y1c, y1s, y3c, y3s, position, sem):
    fill_positions(owner, position)
    my_x, my_core, my_y = place[1], place[2], place[3]
    copies = []

    def copy(source, first, width, target, at):
        copies.append(
            pltpu.make_async_copy(source.at[:, pl.ds(first, width)], target.at[:, pl.ds(at, width)], sem)
        )
        copies[-1].start()

    def flow_x(flow, r, core_to, target, at):
        to_x = my_x ^ r
        block = position[(flow * 4 + to_x) * 2 + core_to]
        copy(d, aligned(block, B), B, target, at)
        chunk = (2 * flow * 4) + to_x * 2 + core_to
        copy(d, pl.multiple_of(32 * B + chunk * EXTRA_CHUNK, EXTRA_CHUNK), EXTRA_CHUNK, target, at + B)

    def flow_y(flow, r, core_to, target, at):
        to_y = my_y ^ r
        for q in range(4):
            block = position[(flow * 4 + (my_x ^ q)) * 2 + core_to]
            copy(d, pl.multiple_of(block * B + to_y * 128, 128), 128, target, at + q * 128)

    def halves(target, at, order):
        for i, h in enumerate(order):
            copy(xb, h * HALF, HALF, target, at + i * HALF)

    def x_message(target, core_to, near, through):
        flow_x(0, near, core_to, target, 0)
        flow_x(1, near, core_to, target, FLOW)
        flow_x(through, 2, core_to, target, 2 * FLOW)
        halves(target, 3 * FLOW, (through, 1 - through))

    def y_message(target, core_to, near, through):
        flow_y(2, near, core_to, target, 0)
        flow_y(3, near, core_to, target, B)
        flow_y(2 + through, 2, core_to, target, 2 * B)
        halves(target, 3 * B, (through, 1 - through))

    other = 1 - my_core
    for x1, x3, y1, y3, to in ((x1c, x3c, y1c, y3c, my_core), (x1s, x3s, y1s, y3s, other)):
        x_message(x1, to, 1, 0)
        x_message(x3, to, 3, 1)
        y_message(y1, to, 1, 0)
        y_message(y3, to, 3, 1)
    for target, to in ((core, other), (own, my_core)):
        flow_x(0, 0, to, target, 0)
        flow_x(1, 0, to, target, FLOW)
        flow_y(2, 0, to, target, 2 * FLOW)
        flow_y(3, 0, to, target, 2 * FLOW + B)
        halves(target, 2 * FLOW + 2 * B, (0, 1))
    for c in copies:
        c.wait()


def pack(owner, place, d, xb):
    rows = d.shape[0]
    widths = [OWN_MSG] * 2 + [X_MSG] * 4 + [Y_MSG] * 4
    return pl.pallas_call(
        pack_kernel,
        out_shape=[jax.ShapeDtypeStruct((rows, w), jnp.bfloat16) for w in widths],
        in_specs=[SMEM, SMEM, ANY, ANY],
        out_specs=[ANY] * len(widths),
        scratch_shapes=[pltpu.SMEM((32,), jnp.int32), pltpu.SemaphoreType.DMA],
        compiler_params=PARAMS,
        name="pack",
    )(owner, place, d, xb)


def contract_rows(a, b):
    return lax.dot_general(a, b, (((0,), (0,)), ((), ())), preferred_element_type=jnp.float32)


def partial_kernel(place, own, core, x1c, x1s, x3c, x3s, y1c, y1s, y3c, y3s, f0, f1, f2, f3,
                   py0, py1, py2, py3, px0, px1, px2, px3, xs, ds, xt, dt):
    my_y = place[3]
    t = own.shape[0]
    end = 2 * FLOW + 2 * B
    for i, ref in enumerate((own, core)):
        rows = pl.ds(i * t, t)
        xs[rows, :] = ref[:, end:]
        xt[rows, :] = ref[:, end:]
        ds[rows, :] = ref[:, : 2 * FLOW]
        dt[rows, :] = ref[:, 2 * FLOW : end]
    for i, ref in enumerate((x1c, x1s, x3c, x3s)):
        rows = pl.ds((2 + i) * t, t)
        ds[rows, :] = ref[:, : 2 * FLOW]
        first = 3 * FLOW
        low, high = (first, first + HALF) if i < 2 else (first + HALF, first)
        xs[rows, :HALF] = ref[:, low : low + HALF]
        xs[rows, HALF:] = ref[:, high : high + HALF]
    for i, ref in enumerate((y1c, y1s, y3c, y3s)):
        rows = pl.ds((2 + i) * t, t)
        dt[rows, :] = ref[:, : 2 * B]
        first = 3 * B
        low, high = (first, first + HALF) if i < 2 else (first + HALF, first)
        xt[rows, :HALF] = ref[:, low : low + HALF]
        xt[rows, HALF:] = ref[:, high : high + HALF]
    rows = pl.ds(6 * t, 2 * t)
    for i, ref in enumerate((f0, f1)):
        ds[rows, i * FLOW : (i + 1) * FLOW] = ref[:, :FLOW]
        xs[rows, i * HALF : (i + 1) * HALF] = ref[:, FLOW:]
    for i, ref in enumerate((f2, f3)):
        dt[rows, i * B : (i + 1) * B] = ref[:, :B]
        xt[rows, i * HALF : (i + 1) * HALF] = ref[:, B:]
    for s, ref in enumerate((py0, py1, py2, py3)):
        features = xs[:, pl.ds(aligned(my_y ^ s, 128), 128)]
        ref[...] = contract_rows(features, ds[...]).astype(ref.dtype)
    for flow in range(2):
        product = contract_rows(xt[...], dt[:, flow * B : (flow + 1) * B])
        for q, ref in enumerate((px0, px1, px2, px3)):
            ref[:, flow * 128 : (flow + 1) * 128] = product[:, q * 128 : (q + 1) * 128].astype(ref.dtype)


def partials(place, pieces):
    t = pieces[0].shape[0]
    kinds = [jnp.float32] + [jnp.bfloat16] * 3
    return pl.pallas_call(
        partial_kernel,
        out_shape=[jax.ShapeDtypeStruct((128, 2 * FLOW), k) for k in kinds]
        + [jax.ShapeDtypeStruct((B, 256), k) for k in kinds],
        in_specs=[SMEM] + [VMEM] * len(pieces),
        out_specs=[VMEM] * 8,
        scratch_shapes=[
            pltpu.VMEM((8 * t, B), jnp.bfloat16),
            pltpu.VMEM((8 * t, 2 * FLOW), jnp.bfloat16),
            pltpu.VMEM((8 * t, B), jnp.bfloat16),
            pltpu.VMEM((8 * t, 2 * B), jnp.bfloat16),
        ],
        compiler_params=PARAMS,
        name="partials",
    )(place, *pieces)


PIECE = 80


def ring_sum_kernel(py0, ry1, ry2, ry3, px0, rx1, rx2, rx3, out):
    wide = py0[...] + ry1[...].astype(jnp.float32) + ry2[...].astype(jnp.float32) + ry3[...].astype(jnp.float32)
    tall = px0[...] + rx1[...].astype(jnp.float32) + rx2[...].astype(jnp.float32) + rx3[...].astype(jnp.float32)
    wide = wide.astype(jnp.bfloat16)
    tall = tall.astype(jnp.bfloat16)
    for z in range(4):
        for low in range(2):
            first = (z * 2 + low) * PIECE
            if z < 2:
                out[first : first + 64, :] = wide[low * 64 : low * 64 + 64, z * FLOW : z * FLOW + B]
            else:
                for g in range(4):
                    from_row = low * 256 + g * 64
                    out[first : first + 64, g * 128 : (g + 1) * 128] = tall[
                        from_row : from_row + 64, (z - 2) * 128 : (z - 1) * 128
                    ]
            k = (z * 2 + low) * 16
            for flow in range(2):
                out[first + 64 : first + PIECE, flow * 128 : (flow + 1) * 128] = wide[
                    k : k + 16, flow * FLOW + B : (flow + 1) * FLOW
                ]
            out[first + 64 : first + PIECE, 256:] = jnp.zeros((16, 256), jnp.bfloat16)


def ring_sum(parts):
    return pl.pallas_call(
        ring_sum_kernel,
        out_shape=jax.ShapeDtypeStruct((8 * PIECE, B), jnp.bfloat16),
        in_specs=[VMEM] * 8,
        out_specs=VMEM,
        compiler_params=PARAMS,
        name="ring_sum",
    )(*parts)


def root_kernel(place, own, far, r1, r2, r3, left_all, right_all, left_rows, right_rows,
                directions, left_new, right_new, g0, g1, a_ref, m_ref):
    my_z, my_y, my_low = place[0], place[3], place[4]
    node = my_y * 2 + my_low
    first_row = aligned(node, 64)
    for r in range(4):
        at_y = my_y ^ r
        for w in range(2):
            at_low = my_low ^ w
            if r == 0:
                piece, base = (own, far)[w], 0
            else:
                piece, base = (r1, r2, r3)[r - 1], w * 128

            @pl.when(my_z < 2)
            def _():
                g0[pl.ds(pl.multiple_of(at_y * 128 + at_low * 64, 64), 64), :] = piece[base : base + 64, :]

            @pl.when(my_z >= 2)
            def _():
                for g in range(4):
                    g0[
                        pl.ds(pl.multiple_of(at_low * 256 + g * 64, 64), 64),
                        pl.ds(aligned(at_y, 128), 128),
                    ] = piece[base : base + 64, g * 128 : (g + 1) * 128]

            for z in range(4):
                g1[pl.ds(pl.multiple_of(at_y * 128 + (z * 2 + at_low) * 16, 16), 16), :] = piece[
                    base + 64 + z * 16 : base + 64 + (z + 1) * 16, :
                ]

    def scaled(gram, statistic, old_rows, new_rows, slot, which):
        a_ref[which] = gram
        rows = a_ref[which, pl.ds(first_row, 64), :]
        new_rows[slot] = BETA * old_rows[slot] + rows * (1.0 / B)
        full = BETA * statistic[slot].astype(jnp.float32) + gram * (1.0 / B)
        norm = B * jnp.sqrt(jnp.sum(full * full, keepdims=True) * (1.0 / (B * B)) + 1e-06)
        matrix = full / norm
        a_ref[which] = matrix
        m_ref[which] = matrix.astype(jnp.bfloat16)
        return lax.rsqrt(jnp.sqrt(norm))

    for slot, g_ref in enumerate((g0, g1)):
        g = g_ref[...]
        left_gram = lax.dot_general(g, g, (((1,), (1,)), ((), ())), preferred_element_type=jnp.float32)
        right_gram = contract_rows(g, g)
        left_scale = scaled(left_gram, left_all, left_rows, left_new, slot, 0)
        right_scale = scaled(right_gram, right_all, right_rows, right_new, slot, 1)
        power = a_ref[0, pl.ds(first_row, 64), :]
        column = lax.broadcasted_iota(jnp.int32, (64, B), 1)
        row = lax.broadcasted_iota(jnp.int32, (64, B), 0) + first_row
        total = jnp.where(row == column, COEF[0], 0.0) + COEF[1] * power
        for k in range(2, 7):
            power = jnp.dot(power.astype(jnp.bfloat16), m_ref[0], preferred_element_type=jnp.float32)
            total = total + COEF[k] * power
        root = (total * left_scale).astype(jnp.bfloat16)
        half = jnp.dot(root, g, preferred_element_type=jnp.float32).astype(jnp.bfloat16)
        power = half.astype(jnp.float32)
        total = COEF[0] * power
        for k in range(1, 7):
            power = jnp.dot(power.astype(jnp.bfloat16), m_ref[1], preferred_element_type=jnp.float32)
            total = total + COEF[k] * power
        directions[slot * 64 : (slot + 1) * 64, :] = (total * right_scale).astype(jnp.bfloat16)


def roots(place, pieces, left_all, right_all, left_rows, right_rows):
    return pl.pallas_call(
        root_kernel,
        out_shape=[
            jax.ShapeDtypeStruct((SLOTS * 64, B), jnp.bfloat16),
            jax.ShapeDtypeStruct((SLOTS, 64, B), jnp.float32),
            jax.ShapeDtypeStruct((SLOTS, 64, B), jnp.float32),
        ],
        in_specs=[SMEM] + [VMEM] * 9,
        out_specs=[VMEM] * 3,
        scratch_shapes=[
            pltpu.VMEM((B, B), jnp.bfloat16),
            pltpu.VMEM((B, B), jnp.bfloat16),
            pltpu.VMEM((2, B, B), jnp.float32),
            pltpu.VMEM((2, B, B), jnp.bfloat16),
        ],
        compiler_params=PARAMS,
        name="roots",
    )(place, *pieces, left_all, right_all, left_rows, right_rows)


def place_kernel(owner, place, *refs):
    sources, out, position, sem = refs[:8], refs[8], refs[9], refs[10]
    fill_positions(owner, position)
    my_z, my_x, my_core = place[0], place[1], place[2]
    for wait in (False, True):
        for flip in range(2):
            for r in range(4):
                source = sources[flip * 4 + r]
                for a in range(4):
                    who = ((my_z ^ a) * 4 + (my_x ^ r)) * 2 + (my_core ^ flip)
                    block = position[who]
                    for slot in range(SLOTS):
                        copy = pltpu.make_async_copy(
                            source.at[pl.ds(a * 128 + slot * 64, 64), :],
                            out.at[:, pl.ds(aligned(jnp.minimum(block + slot * 32, 35), B), B)],
                            sem,
                        )
                        act = copy.wait if wait else copy.start
                        if slot == 0:
                            act()
                        else:
                            pl.when(block < 4)(act)


def put_blocks(owner, place, sources, blocks):
    return pl.pallas_call(
        place_kernel,
        out_shape=jax.ShapeDtypeStruct((64, blocks * B), jnp.bfloat16),
        in_specs=[SMEM, SMEM] + [ANY] * 8,
        out_specs=ANY,
        scratch_shapes=[pltpu.SMEM((32,), jnp.int32), pltpu.SemaphoreType.DMA],
        compiler_params=PARAMS,
        name="put_blocks",
    )(owner, place, *sources)


def shards(x_band, d_gate_up, owner, stat_left, stat_right):
    place = jnp.stack([lax.axis_index(a) for a in FINE]).astype(jnp.int32)
    bucket = d_gate_up.shape[1] // B
    me = lax.axis_index(("z_hi", "x", "core"))
    node_axes = ("y", "z_lo")

    left_all = lax.all_gather(stat_left[0].astype(jnp.bfloat16), node_axes, axis=1, tiled=True)
    right_all = lax.all_gather(stat_right[0].astype(jnp.bfloat16), node_axes, axis=1, tiled=True)

    own, core, x1c, x1s, x3c, x3s, y1c, y1s, y3c, y3s = pack(owner, place, d_gate_up, x_band)
    x1c, x3c = swap(x1c, "x", 1), swap(x3c, "x", 3)
    y1c, y3c = swap(y1c, "y", 1), swap(y3c, "y", 3)
    x1s, x3s = swap_core(x1s, "x", 1), swap_core(x3s, "x", 3)
    y1s, y3s = swap_core(y1s, "y", 1), swap_core(y3s, "y", 3)
    core = swap(core, "core", 1)
    f0 = swap(jnp.concatenate([x1c[:, X_FWD], x1s[:, X_FWD]]), "x", 3)
    f1 = swap(jnp.concatenate([x3c[:, X_FWD], x3s[:, X_FWD]]), "x", 1)
    f2 = swap(jnp.concatenate([y1c[:, Y_FWD], y1s[:, Y_FWD]]), "y", 3)
    f3 = swap(jnp.concatenate([y3c[:, Y_FWD], y3s[:, Y_FWD]]), "y", 1)
    py0, py1, py2, py3, px0, px1, px2, px3 = partials(
        place, (own, core, x1c, x1s, x3c, x3s, y1c, y1s, y3c, y3s, f0, f1, f2, f3)
    )
    ry2, rx2 = swap(py2, "y", 2), swap(px2, "x", 2)
    ry1, rx1 = swap(py1, "y", 1), swap(px1, "x", 1)
    ry3, rx3 = swap(py3, "y", 3), swap(px3, "x", 3)
    message = ring_sum((py0, ry1, ry2, ry3, px0, rx1, rx2, rx3))
    message = lax.all_to_all(message, ("z_hi", "z_lo"), 0, 0, tiled=True)
    summed = jnp.sum(message.reshape(8, PIECE, B).astype(jnp.float32), axis=0).astype(jnp.bfloat16)

    spread = jnp.broadcast_to(summed[64:, :256][None], (32, 16, 256)).reshape(512, 256)
    spread = lax.all_to_all(spread, ("z_hi", "x", "core"), 0, 0, tiled=True)
    mine = jnp.sum(jnp.where(owner[:32] == me, jnp.arange(32, dtype=jnp.int32), 0))
    extra = jnp.minimum(mine, bucket - 33)
    spread = spread.reshape(4, 2, 2, 2, 16, 2, 128)
    chosen = lax.dynamic_slice(spread, (0, extra % 2, 0, 0, 0, extra // 2, 0), (4, 1, 2, 2, 16, 1, 128))
    chosen = chosen.reshape(4, 2, 2, 16, 128).transpose(0, 3, 1, 2, 4).reshape(64, B)
    chosen = jnp.where(mine < bucket - 32, chosen, jnp.zeros_like(chosen))

    mine_rows = jnp.concatenate([summed[:64], chosen])
    far = swap(mine_rows, "z_lo", 1)
    both = jnp.concatenate([mine_rows, far])
    r2, r1, r3 = swap(both, "y", 2), swap(both, "y", 1), swap(both, "y", 3)
    directions, left_new, right_new = roots(
        place, (mine_rows, far, r1, r2, r3), left_all, right_all, stat_left[0], stat_right[0]
    )
    a2, a1, a3 = swap(directions, "z_hi", 2), swap(directions, "z_hi", 1), swap(directions, "z_hi", 3)
    plane = jnp.concatenate([directions, a1, a2, a3])
    b2, b1, b3 = swap(plane, "x", 2), swap(plane, "x", 1), swap(plane, "x", 3)
    near = (plane, b1, b2, b3)
    across = tuple(swap(v, "core", 1) for v in near)
    out = put_blocks(owner, place, near + across, bucket)
    return (out, left_new[None], right_new[None])


def solution(mesh):
    fine = Mesh(np.asarray(mesh.devices).reshape(FINE_SIZES), FINE)
    dp, node = FINE[:3], FINE[3:]
    placed = (P(dp + node, None), P(dp + node, None), P(), P(dp, None, node, None), P(dp, None, node, None))
    return jax.shard_map(
        shards,
        mesh=fine,
        in_specs=placed,
        out_specs=(P(node, None), P(dp, None, node, None), P(dp, None, node, None)),
        check_vma=False,
    )
```

time: 832 us -> 321 us (0.39)
  waiting for transfers between devices: 692 us -> 131 us
  Pallas kernels: 0 us -> 88.6 us
  starting transfers between devices: 0.75 us -> 70.3 us
  matrix products: 58.2 us -> 0 us
  local copies, waits for them, and re-layouts: 47 us -> 10.9 us
  other arithmetic: 10.9 us -> 2.42 us
    psum x1 -> x0, waiting for transfers between devices: 256 us -> none  [shards(): lax.psum(extra_term.astype(jnp.bfloat16), 'dp').astype(jnp.float32)]
    all_gather x4 -> x2, waiting for transfers between devices: 189 us -> 0.01 us  [the longest x1 0.01 us: shards(): lax.all_gather(stat_left[0].astype(jnp.bfloat16), node_axes, axis=1, tile...]
    reduce_scatter x1 -> x0, waiting for transfers between devices: 169 us -> none  [shards(): lax.psum_scatter(contract(x_band, ordered).reshape(B * lax.axis_size('dp'...]
    ppermute x0 -> x33, waiting for transfers between devices: none -> 101 us  [the longest x29 85.4 us: swap(): return lax.ppermute(value, axis, [(i, i ^ mask) for i in range(size)])]
    pallas_call x0 -> x5, Pallas kernels: none -> 88.6 us  [the longest x1 73.2 us: pack(): pl.pallas_call(pack_kernel, out_shape=[jax.ShapeDtypeStruct((rows, w), jn...]
    unnamed x8 -> x2, waiting for transfers between devices: 78.8 us -> 0.03 us
    dot_general x10 -> x0, matrix products: 58.2 us -> none  [the longest x5 37.6 us: batched(): jnp.einsum('kij,kjl->kil', first_matrix, second_matrix, precision=lax.Pre...]
    ppermute x0 -> x33, starting transfers between devices: none -> 55.2 us  [the longest x29 48.4 us: swap(): return lax.ppermute(value, axis, [(i, i ^ mask) for i in range(size)])]
  transfers between devices with their start and end apart: 7 -> 37, of which waited for: 7 -> 21; matrix products, arithmetic and copies ran while one was open for 5% -> 2% of each run, Pallas kernels for 0% -> 2%
where the time goes in v1:
time: 321 us; the launch traced here: 319 us
  waiting for transfers between devices  131 us (41%)
  Pallas kernels  88.6 us (28%)
  starting transfers between devices  70.3 us (22%)
  between operations  15.7 us (5%)
  local copies, waits for them, and re-layouts  10.9 us (3%)
    ppermute x29, waiting for transfers between devices, swap(): return lax.ppermute(value, axis, [(i, i ^ mask) for i in range(size)])  85.4 us
    pallas_call x1, Pallas kernels, pack(): pl.pallas_call(pack_kernel, out_shape=[jax.ShapeDtypeStruct((rows, w), jn...  73.2 us
    ppermute x29, starting transfers between devices, swap(): return lax.ppermute(value, axis, [(i, i ^ mask) for i in range(size)])  48.4 us
    all_to_all x1, waiting for transfers between devices, shards(): message = lax.all_to_all(message, ('z_hi', 'z_lo'), 0, 0, tiled=True)  17 us
    all_to_all x1, waiting for transfers between devices, shards(): spread = lax.all_to_all(spread, ('z_hi', 'x', 'core'), 0, 0, tiled=True)  13.5 us
    ppermute x2, waiting for transfers between devices, swap_core(): return lax.ppermute(value, ('core', 'y'), pairs)  11 us
    all_to_all x1, starting transfers between devices, shards(): message = lax.all_to_all(message, ('z_hi', 'z_lo'), 0, 0, tiled=True)  7.68 us
    all_to_all x1, starting transfers between devices, shards(): spread = lax.all_to_all(spread, ('z_hi', 'x', 'core'), 0, 0, tiled=True)  7.34 us
  transfers between devices with their start and end apart: 37, of which 21 were waited for; matrix products, arithmetic and copies ran while one was open for 2% of the time, Pallas kernels for 2%

profile of v1, /device:TPU:1, one launch (start us, length us, event | category | flops | bytes accessed | tf_op | source)
XLA Modules:
  0.0 319.0 jit_solution(3277771201222556258)
XLA Ops:
  8.9 73.2 %pack.1 = (bf16[128,2816]{1,0:T(8,128)(2,1)S(1)}, bf16[128,2816]{1,0:T(8,128)(2,1)S(1)}, bf16[128,2432]{1,0:T(8,128)(2,1)}, bf16[128,2432]{1,0:T(8,128)(2,1)}, b...) custom-call(s32[36]{0:T(128)S(1)} %copy-done.7, ...), custom_call_target="tpu_custom_call" | custom-call | tf_op jit(solution)/shard_map/pack/pallas_call | solution.py:121
  82.9 2.1 collective-permute-start.5
  85.0 2.7 collective-permute-start.6
  88.8 1.7 collective-permute-start.2
  90.5 4.9 %collective-permute-done.5.y1c = bf16[128,2048]{1,0:T(8,128)(2,1)S(1)} collective-permute-done((bf16[128,2048]{1,0:T(8,128)(2,1)S(1)}, bf16[128,2048]{1,0:T(8,128)(2,1)S(1)}, u32[]{:S(2)}, u32[]{:S(2)}) %collective-permute-start.5) | collective-permute-done | bytes 524320 | tf_op jit(solution)/shard_map/ppermute | solution.py:34
  95.4 2.4 collective-permute-start.1
  97.8 11.0 %collective-permute-done.6.y1s = bf16[128,2048]{1,0:T(8,128)(2,1)S(1)} collective-permute-done((bf16[128,2048]{1,0:T(8,128)(2,1)S(1)}, bf16[128,2048]{1,0:T(8,128)(2,1)S(1)}, u32[]{:S(2)}, u32[]{:S(2)}) %collective-permute-start.6) | collective-permute-done | bytes 524320 | tf_op jit(solution)/shard_map/ppermute | solution.py:43
  108.9 1.9 collective-permute-start.4
  113.2 3.0 collective-permute-start.11
  117.1 2.0 collective-permute-done.1.x1c
  120.1 2.4 collective-permute-start.9
  122.5 4.2 %collective-permute-done.4.x3s = bf16[128,2432]{1,0:T(8,128)(2,1)} collective-permute-done((bf16[128,2432]{1,0:T(8,128)(2,1)}, bf16[128,2432]{1,0:T(8,128)(2,1)}, u32[]{:S(2)}, u32[]{:S(2)}) %collective-permute-start.4) | collective-permute-done | bytes 622624 | tf_op jit(solution)/shard_map/ppermute | solution.py:41
  127.6 11.6 %collective-permute-done.3.x3c = bf16[128,2432]{1,0:T(8,128)(2,1)} collective-permute-done((bf16[128,2432]{1,0:T(8,128)(2,1)}, bf16[128,2432]{1,0:T(8,128)(2,1)}, u32[]{:S(2)}, u32[]{:S(2)}) %collective-permute-start.3) | collective-permute-done | bytes 622624 | tf_op jit(solution)/shard_map/ppermute | solution.py:34
  141.5 10.2 %collective-permute-done.12.f3 = bf16[256,768]{1,0:T(8,128)(2,1)S(1)} collective-permute-done((bf16[256,768]{1,0:T(8,128)(2,1)S(1)}, bf16[256,768]{1,0:T(8,128)(2,1)S(1)}, u32[]{:S(2)}, u32[]{:S(2)}) %collective-permute-start.12) | collective-permute-done | bytes 393248 | tf_op jit(solution)/shard_map/ppermute | solution.py:34
  151.8 5.3 %partials.1 = (f32[128,1280]{1,0:T(8,128)}, bf16[128,1280]{1,0:T(8,128)(2,1)S(1)}, bf16[128,1280]{1,0:T(8,128)(2,1)S(1)}, bf16[128,1280]{1,0:T(8,128)(2,1)S(1)},...) custom-call(s32[5]{0:T(128)S(1)} %stack.23.place, ...), custom_call_target="tpu_custom_call" | custom-call | tf_op jit(solution)/shard_map/partials/pallas_call | solution.py:180
  157.1 1.5 collective-permute-start.16
  158.6 2.3 collective-permute-start.13
  160.9 2.4 collective-permute-start.14
  163.4 2.7 collective-permute-start.18
  166.1 4.1 %collective-permute-done.17.rx2 = bf16[512,256]{1,0:T(8,128)(2,1)S(1)} collective-permute-done((bf16[512,256]{1,0:T(8,128)(2,1)S(1)}, bf16[512,256]{1,0:T(8,128)(2,1)S(1)}, u32[]{:S(2)}, u32[]{:S(2)}) %collective-permute-start.17) | collective-permute-done | bytes 262176 | tf_op jit(solution)/shard_map/ppermute | solution.py:34
  170.2 7.1 %collective-permute-done.18.rx3 = bf16[512,256]{1,0:T(8,128)(2,1)S(1)} collective-permute-done((bf16[512,256]{1,0:T(8,128)(2,1)S(1)}, bf16[512,256]{1,0:T(8,128)(2,1)S(1)}, u32[]{:S(2)}, u32[]{:S(2)}) %collective-permute-start.18) | collective-permute-done | bytes 262176 | tf_op jit(solution)/shard_map/ppermute | solution.py:34
  177.3 1.5 collective-permute-done.15.ry3
  181.0 7.7 %all-to-all-start = ((bf16[8,80,512]{2,1,0:T(8,128)(2,1)}), bf16[8,80,512]{2,1,0:T(8,128)(2,1)S(1)}, u32[]{:S(2)}, u32[]{:S(2)}) async-start(bf16[8,80,512]{2,1,0:T(8,128)(2,1)} %bitcast.5), calls=%async_computation | async-start | bytes 1310720 | tf_op jit(solution)/shard_map/all_to_all | solution.py:383
  189.5 17.0 %all-to-all-done = bf16[8,80,512]{2,1,0:T(8,128)(2,1)S(1)} async-done(((bf16[8,80,512]{2,1,0:T(8,128)(2,1)}), bf16[8,80,512]{2,1,0:T(8,128)(2,1)S(1)}, u32[]{:S(2)}, u32[]{:S(2)}) %all-to-all-start) | async-done | bytes 655392 | tf_op jit(solution)/shard_map/all_to_all | solution.py:383
  207.3 7.3 %all-to-all-start.1 = ((bf16[32,16,256]{2,1,0:T(8,128)(2,1)}), bf16[32,16,256]{2,1,0:T(8,128)(2,1)S(1)}, u32[]{:S(2)}, u32[]{:S(2)}) async-start(bf16[32,16,256]{2,1,0:T(8,128)(2,1)} %broadcast_in_dim.20), calls=%async_computation.1 | async-start | bytes 524288 | tf_op jit(solution)/shard_map/all_to_all | solution.py:387
  216.7 13.5 %all-to-all-done.1 = bf16[32,16,256]{2,1,0:T(8,128)(2,1)S(1)} async-done(((bf16[32,16,256]{2,1,0:T(8,128)(2,1)}), bf16[32,16,256]{2,1,0:T(8,128)(2,1)S(1)}, u32[]{:S(2)}, u32[]{:S(2)}) %all-to-all-start.1) | async-done | bytes 262176 | tf_op jit(solution)/shard_map/all_to_all | solution.py:387
  231.4 6.2 %collective-permute-done.19.far = bf16[128,512]{1,0:T(8,128)(2,1)S(1)} collective-permute-done((bf16[128,512]{1,0:T(8,128)(2,1)S(1)}, bf16[128,512]{1,0:T(8,128)(2,1)S(1)}, u32[]{:S(2)}, u32[]{:S(2)}) %collective-permute-start.19) | collective-permute-done | bytes 131104 | tf_op jit(solution)/shard_map/ppermute | solution.py:34
  237.7 2.7 collective-permute-start.21
  241.6 3.8 %collective-permute-done.20.r1 = bf16[256,512]{1,0:T(8,128)(2,1)S(1)} collective-permute-done((bf16[256,512]{1,0:T(8,128)(2,1)S(1)}, bf16[256,512]{1,0:T(8,128)(2,1)S(1)}, u32[]{:S(2)}, u32[]{:S(2)}) %collective-permute-start.20) | collective-permute-done | bytes 262176 | tf_op jit(solution)/shard_map/ppermute | solution.py:34
  245.4 6.7 %collective-permute-done.21.r2 = bf16[256,512]{1,0:T(8,128)(2,1)S(1)} collective-permute-done((bf16[256,512]{1,0:T(8,128)(2,1)S(1)}, bf16[256,512]{1,0:T(8,128)(2,1)S(1)}, u32[]{:S(2)}, u32[]{:S(2)}) %collective-permute-start.21) | collective-permute-done | bytes 262176 | tf_op jit(solution)/shard_map/ppermute | solution.py:34
  252.1 2.0 collective-permute-done.22.r3
  254.1 1.2 copy-done
  255.3 1.2 copy-done.1
  256.6 7.0 %roots.1 = (bf16[128,512]{1,0:T(8,128)(2,1)S(1)}, f32[2,64,512]{2,1,0:T(8,128)}, f32[2,64,512]{2,1,0:T(8,128)}) custom-call(s32[5]{0:T(128)S(1)} %stack.23.place, bf16[128,512]{1,0:T(8,128)(2,1)S(1)} %pad_maximum_fusion.5.own, bf16[128,512]{1,0:T(8,128)(2,1)S(1)} %collective-permute-done.19.far, bf16[256,512]{1,0:T(8,128)(2,1)S(1)} %collective-permute-done.20.r1, ...), custom_call_target="tpu_custom_call" | custom-call | tf_op jit(solution)/shard_map/roots/pallas_call | solution.py:301
  263.6 2.2 collective-permute-start.23
  265.8 1.4 collective-permute-start.24
  267.2 2.3 collective-permute-start.25
  269.5 6.8 %collective-permute-done.23 = bf16[128,512]{1,0:T(8,128)(2,1)S(1)} collective-permute-done((bf16[128,512]{1,0:T(8,128)(2,1)S(1)}, bf16[128,512]{1,0:T(8,128)(2,1)S(1)}, u32[]{:S(2)}, u32[]{:S(2)}) %collective-permute-start.23) | collective-permute-done | bytes 131104 | tf_op jit(solution)/shard_map/ppermute | solution.py:34
  276.3 1.4 collective-permute-done.24
  279.0 2.9 collective-permute-start.27
  282.8 2.2 collective-permute-start.29
  285.0 6.1 %collective-permute-done.26.refs_1_ = bf16[512,512]{1,0:T(8,128)(2,1)S(1)} collective-permute-done((bf16[512,512]{1,0:T(8,128)(2,1)S(1)}, bf16[512,512]{1,0:T(8,128)(2,1)S(1)}, u32[]{:S(2)}, u32[]{:S(2)}) %collective-permute-start.26) | collective-permute-done | bytes 524320 | tf_op jit(solution)/shard_map/ppermute | solution.py:34
  291.0 4.1 %collective-permute-start.30 = (bf16[512,512]{1,0:T(8,128)(2,1)S(1)}, bf16[512,512]{1,0:T(8,128)(2,1)S(1)}, u32[]{:S(2)}, u32[]{:S(2)}) collective-permute-start(bf16[512,512]{1,0:T(8,128)(2,1)S(1)} %collective-permute-done.26.refs_1_), channel_id=1, source_target_pairs={{0,8},{8,0},{1,9},{9,1},{2,10},{10,2},{3,11},{11,3},{4,12},{12,4},... | collective-permute-start | bytes 1572872 | tf_op jit(solution)/shard_map/ppermute | solution.py:34
  295.1 8.2 %collective-permute-done.27.refs_2_ = bf16[512,512]{1,0:T(8,128)(2,1)S(1)} collective-permute-done((bf16[512,512]{1,0:T(8,128)(2,1)S(1)}, bf16[512,512]{1,0:T(8,128)(2,1)S(1)}, u32[]{:S(2)}, u32[]{:S(2)}) %collective-permute-start.27) | collective-permute-done | bytes 524320 | tf_op jit(solution)/shard_map/ppermute | solution.py:34
  303.3 2.8 collective-permute-start.31
  306.1 2.6 collective-permute-start.32
  308.7 1.5 collective-permute-done.32.refs_7_
  310.2 2.0 put_blocks.1
  (84 shorter events, 20.2 us)
Async XLA Ops:
  7.2 104.4 %copy-start.2 = (f32[1,2,64,512]{3,2,1,0:T(8,128)S(1)}, f32[1,2,64,512]{3,2,1,0:T(8,128)}, u32[]{:S(2)}) copy-start(f32[1,2,64,512]{3,2,1,0:T(8,128)} %param.8) | copy-start | bytes 786436
  7.2 234.4 %all-gather.3.cloned.1.call-start = ((), (), s32[]{:S(2)}) async-start(), calls=%async_computation.2 | async-start | bytes 1179648 | tf_op jit(solution)/shard_map/all_gather | solution.py:363
  7.3 0.9 copy-start.6
  8.2 0.7 copy-start.7
  82.0 0.9 copy-start.4
  82.9 12.5 %collective-permute-start.5 = (bf16[128,2048]{1,0:T(8,128)(2,1)S(1)}, bf16[128,2048]{1,0:T(8,128)(2,1)S(1)}, u32[]{:S(2)}, u32[]{:S(2)}) collective-permute-start(bf16[128,2048]{1,0:T(8,128)(2,1)S(1)} %get-tuple-element.30), channel_id=1, source_target_pairs={{0,2},{2,0},{4,6},{6,4},{1,3},{3,1},{5,7},{7,5},{8,10},{10,8},{12,... | collective-permute-start | bytes 1572872 | tf_op jit(solution)/shard_map/ppermute | solution.py:34
  85.0 23.8 %collective-permute-start.6 = (bf16[128,2048]{1,0:T(8,128)(2,1)S(1)}, bf16[128,2048]{1,0:T(8,128)(2,1)S(1)}, u32[]{:S(2)}, u32[]{:S(2)}) collective-permute-start(bf16[128,2048]{1,0:T(8,128)(2,1)S(1)} %get-tuple-element.31), channel_id=1, source_target_pairs={{0,10},{8,2},{2,8},{10,0},{4,14},{12,6},{6,12},{14,4},{1,11},{9,3}... | collective-permute-start | bytes 1572872 | tf_op jit(solution)/shard_map/ppermute | solution.py:43
  87.8 23.0 %collective-permute-start.8 = (bf16[128,2048]{1,0:T(8,128)(2,1)S(1)}, bf16[128,2048]{1,0:T(8,128)(2,1)S(1)}, u32[]{:S(2)}, u32[]{:S(2)}) collective-permute-start(bf16[128,2048]{1,0:T(8,128)(2,1)S(1)} %get-tuple-element.33), channel_id=1, source_target_pairs={{0,14},{8,6},{2,12},{10,4},{4,10},{12,2},{6,8},{14,0},{1,15},{9,7}... | collective-permute-start | bytes 1572872 | tf_op jit(solution)/shard_map/ppermute | solution.py:43
  88.2 24.1 %collective-permute-start.7 = (bf16[128,2048]{1,0:T(8,128)(2,1)}, bf16[128,2048]{1,0:T(8,128)(2,1)S(1)}, u32[]{:S(2)}, u32[]{:S(2)}) collective-permute-start(bf16[128,2048]{1,0:T(8,128)(2,1)} %get-tuple-element.32), channel_id=1, source_target_pairs={{0,6},{2,4},{4,2},{6,0},{1,7},{3,5},{5,3},{7,1},{8,14},{10,12},{12... | collective-permute-start | bytes 1572872 | tf_op jit(solution)/shard_map/ppermute | solution.py:34
  88.8 24.3 %collective-permute-start.2 = (bf16[128,2432]{1,0:T(8,128)(2,1)}, bf16[128,2432]{1,0:T(8,128)(2,1)}, u32[]{:S(2)}, u32[]{:S(2)}) collective-permute-start(bf16[128,2432]{1,0:T(8,128)(2,1)} %get-tuple-element.27), channel_id=1, source_target_pairs={{0,24},{8,16},{16,8},{24,0},{32,56},{40,48},{48,40},{56,32},{1,25}... | collective-permute-start | bytes 1867784 | tf_op jit(solution)/shard_map/ppermute | solution.py:41
  95.4 23.7 %collective-permute-start.1 = (bf16[128,2432]{1,0:T(8,128)(2,1)}, bf16[128,2432]{1,0:T(8,128)(2,1)}, u32[]{:S(2)}, u32[]{:S(2)}) collective-permute-start(bf16[128,2432]{1,0:T(8,128)(2,1)} %get-tuple-element.26), channel_id=1, source_target_pairs={{0,16},{16,0},{32,48},{48,32},{1,17},{17,1},{33,49},{49,33},{2,18}... | collective-permute-start | bytes 1867784 | tf_op jit(solution)/shard_map/ppermute | solution.py:34
  108.9 17.8 %collective-permute-start.4 = (bf16[128,2432]{1,0:T(8,128)(2,1)}, bf16[128,2432]{1,0:T(8,128)(2,1)}, u32[]{:S(2)}, u32[]{:S(2)}) collective-permute-start(bf16[128,2432]{1,0:T(8,128)(2,1)} %get-tuple-element.29), channel_id=1, source_target_pairs={{0,56},{8,48},{16,40},{24,32},{32,24},{40,16},{48,8},{56,0},{1,57}... | collective-permute-start | bytes 1867784 | tf_op jit(solution)/shard_map/ppermute | solution.py:41
  110.8 28.4 %collective-permute-start.3 = (bf16[128,2432]{1,0:T(8,128)(2,1)}, bf16[128,2432]{1,0:T(8,128)(2,1)}, u32[]{:S(2)}, u32[]{:S(2)}) collective-permute-start(bf16[128,2432]{1,0:T(8,128)(2,1)} %get-tuple-element.28), channel_id=1, source_target_pairs={{0,48},{16,32},{32,16},{48,0},{1,49},{17,33},{33,17},{49,1},{2,50}... | collective-permute-start | bytes 1867784 | tf_op jit(solution)/shard_map/ppermute | solution.py:34
  112.3 29.2 %collective-permute-start = (bf16[128,2816]{1,0:T(8,128)(2,1)S(1)}, bf16[128,2816]{1,0:T(8,128)(2,1)S(1)}, u32[]{:S(2)}, u32[]{:S(2)}) collective-permute-start(bf16[128,2816]{1,0:T(8,128)(2,1)S(1)} %get-tuple-element.25), channel_id=1, source_target_pairs={{0,8},{8,0},{1,9},{9,1},{2,10},{10,2},{3,11},{11,3},{4,12},{12,4},... | collective-permute-start | bytes 2162696 | tf_op jit(solution)/shard_map/ppermute | solution.py:34
  113.2 28.4 %collective-permute-start.11 = (bf16[256,768]{1,0:T(8,128)(2,1)S(1)}, bf16[256,768]{1,0:T(8,128)(2,1)S(1)}, u32[]{:S(2)}, u32[]{:S(2)}) collective-permute-start(bf16[256,768]{1,0:T(8,128)(2,1)S(1)} %pad_maximum_fusion.2), channel_id=1, source_target_pairs={{0,6},{2,4},{4,2},{6,0},{1,7},{3,5},{5,3},{7,1},{8,14},{10,12},{12... | collective-permute-start | bytes 1179656 | tf_op jit(solution)/shard_map/ppermute | solution.py:34
  120.1 31.7 %collective-permute-start.9 = (bf16[256,896]{1,0:T(8,128)(2,1)S(1)}, bf16[256,896]{1,0:T(8,128)(2,1)S(1)}, u32[]{:S(2)}, u32[]{:S(2)}) collective-permute-start(bf16[256,896]{1,0:T(8,128)(2,1)S(1)} %pad_maximum_fusion), channel_id=1, source_target_pairs={{0,48},{16,32},{32,16},{48,0},{1,49},{17,33},{33,17},{49,1},{2,50}... | collective-permute-start | bytes 1376264 | tf_op jit(solution)/shard_map/ppermute | solution.py:34
  140.2 11.6 %collective-permute-start.10 = (bf16[256,896]{1,0:T(8,128)(2,1)S(1)}, bf16[256,896]{1,0:T(8,128)(2,1)S(1)}, u32[]{:S(2)}, u32[]{:S(2)}) collective-permute-start(bf16[256,896]{1,0:T(8,128)(2,1)S(1)} %pad_maximum_fusion.1), channel_id=1, source_target_pairs={{0,16},{16,0},{32,48},{48,32},{1,17},{17,1},{33,49},{49,33},{2,18}... | collective-permute-start | bytes 1376264 | tf_op jit(solution)/shard_map/ppermute | solution.py:34
  140.3 11.4 %collective-permute-start.12 = (bf16[256,768]{1,0:T(8,128)(2,1)S(1)}, bf16[256,768]{1,0:T(8,128)(2,1)S(1)}, u32[]{:S(2)}, u32[]{:S(2)}) collective-permute-start(bf16[256,768]{1,0:T(8,128)(2,1)S(1)} %pad_maximum_fusion.3), channel_id=1, source_target_pairs={{0,2},{2,0},{4,6},{6,4},{1,3},{3,1},{5,7},{7,5},{8,10},{10,8},{12,... | collective-permute-start | bytes 1179656 | tf_op jit(solution)/shard_map/ppermute | solution.py:34
  141.5 10.3 %copy-start.9 = (bf16[128,2816]{1,0:T(8,128)(2,1)}, bf16[128,2816]{1,0:T(8,128)(2,1)S(1)}, u32[]{:S(2)}) copy-start(bf16[128,2816]{1,0:T(8,128)(2,1)S(1)} %collective-permute-done.core) | copy-start | bytes 2162692
  151.8 37.0 %copy-start.3 = (f32[1,2,64,512]{3,2,1,0:T(8,128)S(1)}, f32[1,2,64,512]{3,2,1,0:T(8,128)}, u32[]{:S(2)}) copy-start(f32[1,2,64,512]{3,2,1,0:T(8,128)} %param.9) | copy-start | bytes 786436
  157.1 57.6 %copy-start.8 = (s32[36]{0:T(128)S(1)}, s32[36]{0:T(128)}, u32[]{:S(2)}) copy-start(s32[36]{0:T(128)} %owner.3) | copy-start | bytes 436
  157.1 6.3 %collective-permute-start.16 = (bf16[512,256]{1,0:T(8,128)(2,1)S(1)}, bf16[512,256]{1,0:T(8,128)(2,1)S(1)}, u32[]{:S(2)}, u32[]{:S(2)}) collective-permute-start(bf16[512,256]{1,0:T(8,128)(2,1)S(1)} %get-tuple-element.39), channel_id=1, source_target_pairs={{0,16},{16,0},{32,48},{48,32},{1,17},{17,1},{33,49},{49,33},{2,18}... | collective-permute-start | bytes 786440 | tf_op jit(solution)/shard_map/ppermute | solution.py:34
  158.6 18.7 %collective-permute-start.13 = (bf16[128,1280]{1,0:T(8,128)(2,1)S(1)}, bf16[128,1280]{1,0:T(8,128)(2,1)S(1)}, u32[]{:S(2)}, u32[]{:S(2)}) collective-permute-start(bf16[128,1280]{1,0:T(8,128)(2,1)S(1)} %get-tuple-element.35), channel_id=1, source_target_pairs={{0,2},{2,0},{4,6},{6,4},{1,3},{3,1},{5,7},{7,5},{8,10},{10,8},{12,... | collective-permute-start | bytes 983048 | tf_op jit(solution)/shard_map/ppermute | solution.py:34
  160.9 16.4 %collective-permute-start.14 = (bf16[128,1280]{1,0:T(8,128)(2,1)S(1)}, bf16[128,1280]{1,0:T(8,128)(2,1)S(1)}, u32[]{:S(2)}, u32[]{:S(2)}) collective-permute-start(bf16[128,1280]{1,0:T(8,128)(2,1)S(1)} %get-tuple-element.36), channel_id=1, source_target_pairs={{0,4},{2,6},{4,0},{6,2},{1,5},{3,7},{5,1},{7,3},{8,12},{10,14},{12... | collective-permute-start | bytes 983048 | tf_op jit(solution)/shard_map/ppermute | solution.py:34
  163.4 15.5 %collective-permute-start.15 = (bf16[128,1280]{1,0:T(8,128)(2,1)S(1)}, bf16[128,1280]{1,0:T(8,128)(2,1)S(1)}, u32[]{:S(2)}, u32[]{:S(2)}) collective-permute-start(bf16[128,1280]{1,0:T(8,128)(2,1)S(1)} %get-tuple-element.37), channel_id=1, source_target_pairs={{0,6},{2,4},{4,2},{6,0},{1,7},{3,5},{5,3},{7,1},{8,14},{10,12},{12... | collective-permute-start | bytes 983048 | tf_op jit(solution)/shard_map/ppermute | solution.py:34
  163.4 6.8 %collective-permute-start.17 = (bf16[512,256]{1,0:T(8,128)(2,1)S(1)}, bf16[512,256]{1,0:T(8,128)(2,1)S(1)}, u32[]{:S(2)}, u32[]{:S(2)}) collective-permute-start(bf16[512,256]{1,0:T(8,128)(2,1)S(1)} %get-tuple-element.40), channel_id=1, source_target_pairs={{0,32},{16,48},{32,0},{48,16},{1,33},{17,49},{33,1},{49,17},{2,34}... | collective-permute-start | bytes 786440 | tf_op jit(solution)/shard_map/ppermute | solution.py:34
  163.4 13.9 %collective-permute-start.18 = (bf16[512,256]{1,0:T(8,128)(2,1)S(1)}, bf16[512,256]{1,0:T(8,128)(2,1)S(1)}, u32[]{:S(2)}, u32[]{:S(2)}) collective-permute-start(bf16[512,256]{1,0:T(8,128)(2,1)S(1)} %get-tuple-element.41), channel_id=1, source_target_pairs={{0,48},{16,32},{32,16},{48,0},{1,49},{17,33},{33,17},{49,1},{2,50}... | collective-permute-start | bytes 786440 | tf_op jit(solution)/shard_map/ppermute | solution.py:34
  178.8 1.1 copy-start.5
  181.0 25.5 %all-to-all-start = ((bf16[8,80,512]{2,1,0:T(8,128)(2,1)}), bf16[8,80,512]{2,1,0:T(8,128)(2,1)S(1)}, u32[]{:S(2)}, u32[]{:S(2)}) async-start(bf16[8,80,512]{2,1,0:T(8,128)(2,1)} %bitcast.5), calls=%async_computation | async-start | bytes 1310720 | tf_op jit(solution)/shard_map/all_to_all | solution.py:383
  188.7 52.9 %all-gather.5.cloned.1.call-start = ((), (), s32[]{:S(2)}) async-start(), calls=%async_computation.3 | async-start | bytes 1179648 | tf_op jit(solution)/shard_map/all_gather | solution.py:364
  207.3 22.8 %all-to-all-start.1 = ((bf16[32,16,256]{2,1,0:T(8,128)(2,1)}), bf16[32,16,256]{2,1,0:T(8,128)(2,1)S(1)}, u32[]{:S(2)}, u32[]{:S(2)}) async-start(bf16[32,16,256]{2,1,0:T(8,128)(2,1)} %broadcast_in_dim.20), calls=%async_computation.1 | async-start | bytes 524288 | tf_op jit(solution)/shard_map/all_to_all | solution.py:387
  230.6 7.0 %collective-permute-start.19 = (bf16[128,512]{1,0:T(8,128)(2,1)S(1)}, bf16[128,512]{1,0:T(8,128)(2,1)S(1)}, u32[]{:S(2)}, u32[]{:S(2)}) collective-permute-start(bf16[128,512]{1,0:T(8,128)(2,1)S(1)} %pad_maximum_fusion.5.own), channel_id=1, source_target_pairs={{0,1},{1,0},{2,3},{3,2},{4,5},{5,4},{6,7},{7,6},{8,9},{9,8},{10,11... | collective-permute-start | bytes 393224 | tf_op jit(solution)/shard_map/ppermute | solution.py:34
  237.6 7.8 %collective-permute-start.20 = (bf16[256,512]{1,0:T(8,128)(2,1)S(1)}, bf16[256,512]{1,0:T(8,128)(2,1)S(1)}, u32[]{:S(2)}, u32[]{:S(2)}) collective-permute-start(bf16[256,512]{1,0:T(8,128)(2,1)S(1)} %pad_maximum_fusion.4), channel_id=1, source_target_pairs={{0,2},{2,0},{4,6},{6,4},{1,3},{3,1},{5,7},{7,5},{8,10},{10,8},{12,... | collective-permute-start | bytes 786440 | tf_op jit(solution)/shard_map/ppermute | solution.py:34
  237.7 14.4 %collective-permute-start.21 = (bf16[256,512]{1,0:T(8,128)(2,1)S(1)}, bf16[256,512]{1,0:T(8,128)(2,1)S(1)}, u32[]{:S(2)}, u32[]{:S(2)}) collective-permute-start(bf16[256,512]{1,0:T(8,128)(2,1)S(1)} %pad_maximum_fusion.4), channel_id=1, source_target_pairs={{0,4},{2,6},{4,0},{6,2},{1,5},{3,7},{5,1},{7,3},{8,12},{10,14},{12... | collective-permute-start | bytes 786440 | tf_op jit(solution)/shard_map/ppermute | solution.py:34
  240.4 13.7 %collective-permute-start.22 = (bf16[256,512]{1,0:T(8,128)(2,1)S(1)}, bf16[256,512]{1,0:T(8,128)(2,1)S(1)}, u32[]{:S(2)}, u32[]{:S(2)}) collective-permute-start(bf16[256,512]{1,0:T(8,128)(2,1)S(1)} %pad_maximum_fusion.4), channel_id=1, source_target_pairs={{0,6},{2,4},{4,2},{6,0},{1,7},{3,5},{5,3},{7,1},{8,14},{10,12},{12... | collective-permute-start | bytes 786440 | tf_op jit(solution)/shard_map/ppermute | solution.py:34
  254.1 1.2 copy-start
  255.3 1.2 copy-start.1
  263.6 12.6 %collective-permute-start.23 = (bf16[128,512]{1,0:T(8,128)(2,1)S(1)}, bf16[128,512]{1,0:T(8,128)(2,1)S(1)}, u32[]{:S(2)}, u32[]{:S(2)}) collective-permute-start(bf16[128,512]{1,0:T(8,128)(2,1)S(1)} %get-tuple-element.42), channel_id=1, source_target_pairs={{0,64},{64,0},{128,192},{192,128},{1,65},{65,1},{129,193},{193,129... | collective-permute-start | bytes 393224 | tf_op jit(solution)/shard_map/ppermute | solution.py:34
  265.8 11.9 %collective-permute-start.24 = (bf16[128,512]{1,0:T(8,128)(2,1)S(1)}, bf16[128,512]{1,0:T(8,128)(2,1)S(1)}, u32[]{:S(2)}, u32[]{:S(2)}) collective-permute-start(bf16[128,512]{1,0:T(8,128)(2,1)S(1)} %get-tuple-element.42), channel_id=1, source_target_pairs={{0,128},{64,192},{128,0},{192,64},{1,129},{65,193},{129,1},{193,65... | collective-permute-start | bytes 393224 | tf_op jit(solution)/shard_map/ppermute | solution.py:34
  267.2 11.6 %collective-permute-start.25 = (bf16[128,512]{1,0:T(8,128)(2,1)S(1)}, bf16[128,512]{1,0:T(8,128)(2,1)S(1)}, u32[]{:S(2)}, u32[]{:S(2)}) collective-permute-start(bf16[128,512]{1,0:T(8,128)(2,1)S(1)} %get-tuple-element.42), channel_id=1, source_target_pairs={{0,192},{64,128},{128,64},{192,0},{1,193},{65,129},{129,65},{193,1... | collective-permute-start | bytes 393224 | tf_op jit(solution)/shard_map/ppermute | solution.py:34
  278.9 12.2 %collective-permute-start.26 = (bf16[512,512]{1,0:T(8,128)(2,1)S(1)}, bf16[512,512]{1,0:T(8,128)(2,1)S(1)}, u32[]{:S(2)}, u32[]{:S(2)}) collective-permute-start(bf16[512,512]{1,0:T(8,128)(2,1)S(1)} %constant_dynamic-update-slice_fusion.refs_0_), channel_id=1, source_target_pairs={{0,16},{16,0},{32,48},{48,32},{1,17},{17,1},{33,49},{49,33},{2,18}... | collective-permute-start | bytes 1572872 | tf_op jit(solution)/shard_map/ppermute | solution.py:34
  279.0 24.3 %collective-permute-start.27 = (bf16[512,512]{1,0:T(8,128)(2,1)S(1)}, bf16[512,512]{1,0:T(8,128)(2,1)S(1)}, u32[]{:S(2)}, u32[]{:S(2)}) collective-permute-start(bf16[512,512]{1,0:T(8,128)(2,1)S(1)} %constant_dynamic-update-slice_fusion.refs_0_), channel_id=1, source_target_pairs={{0,32},{16,48},{32,0},{48,16},{1,33},{17,49},{33,1},{49,17},{2,34}... | collective-permute-start | bytes 1572872 | tf_op jit(solution)/shard_map/ppermute | solution.py:34
  281.9 24.2 %collective-permute-start.28 = (bf16[512,512]{1,0:T(8,128)(2,1)S(1)}, bf16[512,512]{1,0:T(8,128)(2,1)S(1)}, u32[]{:S(2)}, u32[]{:S(2)}) collective-permute-start(bf16[512,512]{1,0:T(8,128)(2,1)S(1)} %constant_dynamic-update-slice_fusion.refs_0_), channel_id=1, source_target_pairs={{0,48},{16,32},{32,16},{48,0},{1,49},{17,33},{33,17},{49,1},{2,50}... | collective-permute-start | bytes 1572872 | tf_op jit(solution)/shard_map/ppermute | solution.py:34
  282.8 25.8 %collective-permute-start.29 = (bf16[512,512]{1,0:T(8,128)(2,1)S(1)}, bf16[512,512]{1,0:T(8,128)(2,1)S(1)}, u32[]{:S(2)}, u32[]{:S(2)}) collective-permute-start(bf16[512,512]{1,0:T(8,128)(2,1)S(1)} %constant_dynamic-update-slice_fusion.refs_0_), channel_id=1, source_target_pairs={{0,8},{8,0},{1,9},{9,1},{2,10},{10,2},{3,11},{11,3},{4,12},{12,4},... | collective-permute-start | bytes 1572872 | tf_op jit(solution)/shard_map/ppermute | solution.py:34
  291.0 17.6 %collective-permute-start.30 = (bf16[512,512]{1,0:T(8,128)(2,1)S(1)}, bf16[512,512]{1,0:T(8,128)(2,1)S(1)}, u32[]{:S(2)}, u32[]{:S(2)}) collective-permute-start(bf16[512,512]{1,0:T(8,128)(2,1)S(1)} %collective-permute-done.26.refs_1_), channel_id=1, source_target_pairs={{0,8},{8,0},{1,9},{9,1},{2,10},{10,2},{3,11},{11,3},{4,12},{12,4},... | collective-permute-start | bytes 1572872 | tf_op jit(solution)/shard_map/ppermute | solution.py:34
  303.3 5.4 %collective-permute-start.31 = (bf16[512,512]{1,0:T(8,128)(2,1)S(1)}, bf16[512,512]{1,0:T(8,128)(2,1)S(1)}, u32[]{:S(2)}, u32[]{:S(2)}) collective-permute-start(bf16[512,512]{1,0:T(8,128)(2,1)S(1)} %collective-permute-done.27.refs_2_), channel_id=1, source_target_pairs={{0,8},{8,0},{1,9},{9,1},{2,10},{10,2},{3,11},{11,3},{4,12},{12,4},... | collective-permute-start | bytes 1572872 | tf_op jit(solution)/shard_map/ppermute | solution.py:34
  306.1 4.1 %collective-permute-start.32 = (bf16[512,512]{1,0:T(8,128)(2,1)S(1)}, bf16[512,512]{1,0:T(8,128)(2,1)S(1)}, u32[]{:S(2)}, u32[]{:S(2)}) collective-permute-start(bf16[512,512]{1,0:T(8,128)(2,1)S(1)} %collective-permute-done.28.refs_3_), channel_id=1, source_target_pairs={{0,8},{8,0},{1,9},{9,1},{2,10},{10,2},{3,11},{11,3},{4,12},{12,4},... | collective-permute-start | bytes 1572872 | tf_op jit(solution)/shard_map/ppermute | solution.py:34
Sparse Core Ops, SparseCore 0:
  112.4 41.3 all-gather.2
  191.4 44.7 all-gather.4

commit v2 on v1

v2 whole, which is shorter than its diff:
```python
import functools
import math

import jax
import jax.numpy as jnp
import numpy as np
from jax import lax
from jax.experimental import pallas as pl
from jax.experimental.pallas import tpu as pltpu
from jax.sharding import Mesh, PartitionSpec as P

B = 512
SLOTS = 2
BETA = 0.9
EXTRA_CHUNK = 128
FLOW = B + EXTRA_CHUNK
HALF = B // 2

FINE = ("z_hi", "x", "core", "y", "z_lo")
FINE_SIZES = (4, 4, 2, 4, 2)
VMEM_LIMIT = 24 * 1024 * 1024

COEF = [6.25 / 4, -(1.25 + 1.25**5) / 4] + [
    -math.comb(5, k) * 1.25 ** (5 - k) * (-0.25) ** k / 4 for k in range(1, 6)
]

ANY = pl.BlockSpec(memory_space=pl.ANY)
SMEM = pl.BlockSpec(memory_space=pltpu.SMEM)
VMEM = pl.BlockSpec(memory_space=pltpu.VMEM)
PARAMS = pltpu.CompilerParams(vmem_limit_bytes=VMEM_LIMIT)


def swap(value, axis, mask):
    size = FINE_SIZES[FINE.index(axis)]
    return lax.ppermute(value, axis, [(i, i ^ mask) for i in range(size)])


def aligned(index, step):
    return pl.multiple_of(index * step, step)


def fill_positions(owner, position):
    for block in range(32):
        position[owner[block]] = block


X_DIRECT = 4 * FLOW
X_MSG = 6 * FLOW + B
Y_DIRECT = 4 * B
Y_MSG = 6 * B + B
OWN_MSG = 4 * FLOW + 4 * B
X_FWD = slice(X_DIRECT, 6 * FLOW + HALF)
Y_FWD = slice(Y_DIRECT, 6 * B + HALF)


class Packer:
    def __init__(self, owner, place, d, position, sem):
        fill_positions(owner, position)
        self.position, self.place, self.d, self.sem = position, place, d, sem
        self.cores = (place[2], 1 - place[2])
        self.copies = []

    def copy(self, source, first, width, target, at):
        self.copies.append(
            pltpu.make_async_copy(source.at[:, pl.ds(first, width)], target.at[:, pl.ds(at, width)], self.sem)
        )
        self.copies[-1].start()

    def flow_x(self, flow, r, core, target, at):
        to_x = self.place[1] ^ r
        block = self.position[(flow * 4 + to_x) * 2 + core]
        self.copy(self.d, aligned(block, B), B, target, at)
        chunk = 32 * B // EXTRA_CHUNK + flow * 8 + to_x * 2 + core
        self.copy(self.d, aligned(chunk, EXTRA_CHUNK), EXTRA_CHUNK, target, at + B)

    def flow_y(self, flow, r, core, target, at):
        to_y = self.place[3] ^ r
        for q in range(4):
            block = self.position[(flow * 4 + (self.place[1] ^ q)) * 2 + core]
            self.copy(self.d, pl.multiple_of(block * B + to_y * 128, 128), 128, target, at + q * 128)

    def finish(self):
        for c in self.copies:
            c.wait()


def pack_kernel(owner, place, d, xb, x1, x3, y1, y3, position, sem):
    packer = Packer(owner, place, d, position, sem)
    for near, through, on_x, on_y in ((1, 0, x1, y1), (3, 1, x3, y3)):
        for i, core in enumerate(packer.cores):
            packer.flow_x(0, near, core, on_x, i * 2 * FLOW)
            packer.flow_x(1, near, core, on_x, i * 2 * FLOW + FLOW)
            packer.flow_x(through, 2, core, on_x, X_DIRECT + i * FLOW)
            packer.flow_y(2, near, core, on_y, i * 2 * B)
            packer.flow_y(3, near, core, on_y, i * 2 * B + B)
            packer.flow_y(2 + through, 2, core, on_y, Y_DIRECT + i * B)
        for i, h in enumerate((through, 1 - through)):
            packer.copy(xb, h * HALF, HALF, on_x, 6 * FLOW + i * HALF)
            packer.copy(xb, h * HALF, HALF, on_y, 6 * B + i * HALF)
    packer.finish()


def pack_own_kernel(owner, place, d, out, position, sem):
    packer = Packer(owner, place, d, position, sem)
    for i, core in enumerate(packer.cores):
        for flow in range(2):
            packer.flow_x(flow, 0, core, out, (i * 2 + flow) * FLOW)
            packer.flow_y(2 + flow, 0, core, out, 4 * FLOW + (i * 2 + flow) * B)
    packer.finish()


def packed(kernel, name, widths, owner, place, d, *more):
    rows = d.shape[0]
    return pl.pallas_call(
        kernel,
        out_shape=[jax.ShapeDtypeStruct((rows, w), jnp.bfloat16) for w in widths],
        in_specs=[SMEM, SMEM, ANY] + [ANY] * len(more),
        out_specs=[VMEM] * len(widths),
        scratch_shapes=[pltpu.SMEM((32,), jnp.int32), pltpu.SemaphoreType.DMA],
        compiler_params=PARAMS,
        name=name,
    )(owner, place, d, *more)


def contract_rows(a, b):
    return lax.dot_general(a, b, (((0,), (0,)), ((), ())), preferred_element_type=jnp.float32)


def partial_kernel(which, own, xb, x1, x3, y1, y3, f0, f1, f2, f3, wide, tall, xs, ds, xt, dt):
    t = own.shape[0]
    wide_at = which * 2 * FLOW
    tall_at = which * 2 * B
    rows = pl.ds(0, t)
    xs[rows, :] = xb[...]
    xt[rows, :] = xb[...]
    ds[rows, :] = own[:, wide_at : wide_at + 2 * FLOW]
    dt[rows, :] = own[:, 4 * FLOW + tall_at : 4 * FLOW + tall_at + 2 * B]
    for i, (on_x, on_y) in enumerate(((x1, y1), (x3, y3))):
        rows = pl.ds((1 + i) * t, t)
        ds[rows, :] = on_x[:, wide_at : wide_at + 2 * FLOW]
        dt[rows, :] = on_y[:, tall_at : tall_at + 2 * B]
        for k, h in enumerate((i, 1 - i)):
            xs[rows, h * HALF : (h + 1) * HALF] = on_x[:, 6 * FLOW + k * HALF : 6 * FLOW + (k + 1) * HALF]
            xt[rows, h * HALF : (h + 1) * HALF] = on_y[:, 6 * B + k * HALF : 6 * B + (k + 1) * HALF]
    rows = pl.ds(3 * t, t)
    for i, (on_x, on_y) in enumerate(((f0, f2), (f1, f3))):
        ds[rows, i * FLOW : (i + 1) * FLOW] = on_x[:, which * FLOW : (which + 1) * FLOW]
        dt[rows, i * B : (i + 1) * B] = on_y[:, which * B : (which + 1) * B]
        xs[rows, i * HALF : (i + 1) * HALF] = on_x[:, 2 * FLOW :]
        xt[rows, i * HALF : (i + 1) * HALF] = on_y[:, 2 * B :]
    wide[...] = contract_rows(xs[...], ds[...]).astype(wide.dtype)
    tall[...] = contract_rows(xt[...], dt[...]).astype(tall.dtype)


def partials(which, pieces):
    t = pieces[0].shape[0]
    return pl.pallas_call(
        functools.partial(partial_kernel, which),
        out_shape=[
            jax.ShapeDtypeStruct((B, 2 * FLOW), jnp.bfloat16),
            jax.ShapeDtypeStruct((B, 2 * B), jnp.bfloat16),
        ],
        in_specs=[VMEM] * len(pieces),
        out_specs=[VMEM] * 2,
        scratch_shapes=[
            pltpu.VMEM((4 * t, B), jnp.bfloat16),
            pltpu.VMEM((4 * t, 2 * FLOW), jnp.bfloat16),
            pltpu.VMEM((4 * t, B), jnp.bfloat16),
            pltpu.VMEM((4 * t, 2 * B), jnp.bfloat16),
        ],
        compiler_params=PARAMS,
        name="partials",
    )(*pieces)


def chip_sum_kernel(place, wide, tall, far_wide, far_tall, py0, py1, py2, py3, px0, px1, px2, px3):
    my_y = place[3]
    for s, ref in enumerate((py0, py1, py2, py3)):
        rows = pl.ds(aligned(my_y ^ s, 128), 128)
        ref[...] = (wide[rows, :].astype(jnp.float32) + far_wide[rows, :].astype(jnp.float32)).astype(ref.dtype)
    for q, ref in enumerate((px0, px1, px2, px3)):
        for flow in range(2):
            at = flow * B + q * 128
            ref[:, flow * 128 : (flow + 1) * 128] = (
                tall[:, at : at + 128].astype(jnp.float32) + far_tall[:, at : at + 128].astype(jnp.float32)
            ).astype(ref.dtype)


def chip_sum(place, *parts):
    kinds = [jnp.float32] + [jnp.bfloat16] * 3
    return pl.pallas_call(
        chip_sum_kernel,
        out_shape=[jax.ShapeDtypeStruct((128, 2 * FLOW), k) for k in kinds]
        + [jax.ShapeDtypeStruct((B, 256), k) for k in kinds],
        in_specs=[SMEM] + [VMEM] * 4,
        out_specs=[VMEM] * 8,
        compiler_params=PARAMS,
        name="chip_sum",
    )(place, *parts)


PIECE = 80


def ring_sum_kernel(py0, ry1, ry2, ry3, px0, rx1, rx2, rx3, out):
    wide = py0[...] + ry1[...].astype(jnp.float32) + ry2[...].astype(jnp.float32) + ry3[...].astype(jnp.float32)
    tall = px0[...] + rx1[...].astype(jnp.float32) + rx2[...].astype(jnp.float32) + rx3[...].astype(jnp.float32)
    wide = wide.astype(jnp.bfloat16)
    tall = tall.astype(jnp.bfloat16)
    for z in range(4):
        for low in range(2):
            first = (z * 2 + low) * PIECE
            if z < 2:
                out[first : first + 64, :] = wide[low * 64 : low * 64 + 64, z * FLOW : z * FLOW + B]
            else:
                for g in range(4):
                    from_row = low * 256 + g * 64
                    out[first : first + 64, g * 128 : (g + 1) * 128] = tall[
                        from_row : from_row + 64, (z - 2) * 128 : (z - 1) * 128
                    ]
            k = (z * 2 + low) * 16
            for flow in range(2):
                out[first + 64 : first + PIECE, flow * 128 : (flow + 1) * 128] = wide[
                    k : k + 16, flow * FLOW + B : (flow + 1) * FLOW
                ]
            out[first + 64 : first + PIECE, 256:] = jnp.zeros((16, 256), jnp.bfloat16)


def ring_sum(parts):
    return pl.pallas_call(
        ring_sum_kernel,
        out_shape=jax.ShapeDtypeStruct((8 * PIECE, B), jnp.bfloat16),
        in_specs=[VMEM] * 8,
        out_specs=VMEM,
        compiler_params=PARAMS,
        name="ring_sum",
    )(*parts)


def line_sum_kernel(arrived, main, spread):
    total = arrived[0].astype(jnp.float32)
    for i in range(1, 8):
        total = total + arrived[i].astype(jnp.float32)
    total = total.astype(jnp.bfloat16)
    main[...] = total[:64]
    for i in range(64):
        spread[i * 16 : (i + 1) * 16, :] = total[64:, :256]


def line_sum(arrived):
    return pl.pallas_call(
        line_sum_kernel,
        out_shape=[jax.ShapeDtypeStruct((64, B), jnp.bfloat16), jax.ShapeDtypeStruct((64 * 16, 256), jnp.bfloat16)],
        in_specs=[VMEM],
        out_specs=[VMEM] * 2,
        compiler_params=PARAMS,
        name="line_sum",
    )(arrived)


def choose_kernel(owner, place, main, far, spread, out, position):
    fill_positions(owner, position)
    mine = position[(place[0] * 4 + place[1]) * 2 + place[2]]
    out[:64, :] = main[...]
    out[64:128, :] = far[...]

    @pl.when(mine >= 4)
    def _():
        out[128:, :] = jnp.zeros((128, B), jnp.bfloat16)

    @pl.when(mine < 4)
    def _():
        lanes = pl.ds(aligned(mine >> 1, 128), 128)
        for z in range(4):
            for xl in range(2):
                for core in range(2):
                    for low in range(2):
                        source = (((z * 4 + 2 * (mine & 1) + xl) * 2 + core) * 2 + low) * 16
                        to = 128 + low * 64 + z * 16
                        at = (xl * 2 + core) * 128
                        out[to : to + 16, at : at + 128] = spread[pl.ds(pl.multiple_of(source, 16), 16), lanes]


def choose(owner, place, main, far, spread):
    return pl.pallas_call(
        choose_kernel,
        out_shape=jax.ShapeDtypeStruct((256, B), jnp.bfloat16),
        in_specs=[SMEM, SMEM] + [VMEM] * 3,
        out_specs=VMEM,
        scratch_shapes=[pltpu.SMEM((32,), jnp.int32)],
        compiler_params=PARAMS,
        name="choose",
    )(owner, place, main, far, spread)


def root_kernel(place, r0, r1, r2, r3, statistics, left_rows, right_rows,
                directions, left_new, right_new, g0, g1, a_ref, m_ref):
    my_z, my_y, my_low = place[0], place[3], place[4]
    node = my_y * 2 + my_low
    first_row = aligned(node, 64)
    for r, piece in enumerate((r0, r1, r2, r3)):
        at_y = my_y ^ r
        for w in range(2):
            at_low = my_low ^ w
            base = w * 64

            @pl.when(my_z < 2)
            def _():
                g0[pl.ds(pl.multiple_of(at_y * 128 + at_low * 64, 64), 64), :] = piece[base : base + 64, :]

            @pl.when(my_z >= 2)
            def _():
                for g in range(4):
                    g0[
                        pl.ds(pl.multiple_of(at_low * 256 + g * 64, 64), 64),
                        pl.ds(aligned(at_y, 128), 128),
                    ] = piece[base : base + 64, g * 128 : (g + 1) * 128]

            for z in range(4):
                g1[pl.ds(pl.multiple_of(at_y * 128 + (z * 2 + w) * 16, 16), 16), :] = piece[
                    128 + w * 64 + z * 16 : 128 + w * 64 + (z + 1) * 16, :
                ]

    def scaled(gram, old_rows, new_rows, slot, which):
        a_ref[which] = gram
        rows = a_ref[which, pl.ds(first_row, 64), :]
        new_rows[slot] = BETA * old_rows[slot] + rows * (1.0 / B)
        full = BETA * statistics[which * SLOTS + slot].astype(jnp.float32) + gram * (1.0 / B)
        norm = B * jnp.sqrt(jnp.sum(full * full, keepdims=True) * (1.0 / (B * B)) + 1e-06)
        matrix = full / norm
        a_ref[which] = matrix
        m_ref[which] = matrix.astype(jnp.bfloat16)
        return lax.rsqrt(jnp.sqrt(norm))

    for slot, g_ref in enumerate((g0, g1)):
        g = g_ref[...]
        left_gram = lax.dot_general(g, g, (((1,), (1,)), ((), ())), preferred_element_type=jnp.float32)
        right_gram = contract_rows(g, g)
        left_scale = scaled(left_gram, left_rows, left_new, slot, 0)
        right_scale = scaled(right_gram, right_rows, right_new, slot, 1)
        power = a_ref[0, pl.ds(first_row, 64), :]
        column = lax.broadcasted_iota(jnp.int32, (64, B), 1)
        row = lax.broadcasted_iota(jnp.int32, (64, B), 0) + first_row
        total = jnp.where(row == column, COEF[0], 0.0) + COEF[1] * power
        for k in range(2, 7):
            power = jnp.dot(power.astype(jnp.bfloat16), m_ref[0], preferred_element_type=jnp.float32)
            total = total + COEF[k] * power
        root = (total * left_scale).astype(jnp.bfloat16)
        half = jnp.dot(root, g, preferred_element_type=jnp.float32).astype(jnp.bfloat16)
        power = half.astype(jnp.float32)
        total = COEF[0] * power
        for k in range(1, 7):
            power = jnp.dot(power.astype(jnp.bfloat16), m_ref[1], preferred_element_type=jnp.float32)
            total = total + COEF[k] * power
        directions[slot * 64 : (slot + 1) * 64, :] = (total * right_scale).astype(jnp.bfloat16)


def roots(place, pieces, statistics, left_rows, right_rows):
    return pl.pallas_call(
        root_kernel,
        out_shape=[
            jax.ShapeDtypeStruct((SLOTS * 64, B), jnp.bfloat16),
            jax.ShapeDtypeStruct((SLOTS, 64, B), jnp.float32),
            jax.ShapeDtypeStruct((SLOTS, 64, B), jnp.float32),
        ],
        in_specs=[SMEM] + [VMEM] * 7,
        out_specs=[VMEM] * 3,
        scratch_shapes=[
            pltpu.VMEM((B, B), jnp.bfloat16),
            pltpu.VMEM((B, B), jnp.bfloat16),
            pltpu.VMEM((2, B, B), jnp.float32),
            pltpu.VMEM((2, B, B), jnp.bfloat16),
        ],
        compiler_params=PARAMS,
        name="roots",
    )(place, *pieces, statistics, left_rows, right_rows)


def place_kernel(owner, place, *refs):
    sources, out, position, sem = refs[:8], refs[8], refs[9], refs[10]
    fill_positions(owner, position)
    my_z, my_x, my_core = place[0], place[1], place[2]
    for wait in (False, True):
        for flip in range(2):
            for r in range(4):
                source = sources[flip * 4 + r]
                for a in range(4):
                    who = ((my_z ^ a) * 4 + (my_x ^ r)) * 2 + (my_core ^ flip)
                    block = position[who]
                    for slot in range(SLOTS):
                        copy = pltpu.make_async_copy(
                            source.at[pl.ds(a * 128 + slot * 64, 64), :],
                            out.at[:, pl.ds(aligned(jnp.minimum(block + slot * 32, 35), B), B)],
                            sem,
                        )
                        act = copy.wait if wait else copy.start
                        if slot == 0:
                            act()
                        else:
                            pl.when(block < 4)(act)


def put_blocks(owner, place, sources, blocks):
    return pl.pallas_call(
        place_kernel,
        out_shape=jax.ShapeDtypeStruct((64, blocks * B), jnp.bfloat16),
        in_specs=[SMEM, SMEM] + [ANY] * 8,
        out_specs=ANY,
        scratch_shapes=[pltpu.SMEM((32,), jnp.int32), pltpu.SemaphoreType.DMA],
        compiler_params=PARAMS,
        name="put_blocks",
    )(owner, place, *sources)


def shards(x_band, d_gate_up, owner, stat_left, stat_right):
    place = jnp.stack([lax.axis_index(a) for a in FINE]).astype(jnp.int32)
    bucket = d_gate_up.shape[1] // B
    statistics = jnp.concatenate([stat_left[0], stat_right[0]]).astype(jnp.bfloat16)
    statistics = lax.all_gather(statistics, ("y", "z_lo"), axis=1, tiled=True)

    x1, x3, y1, y3 = packed(pack_kernel, "pack", [X_MSG] * 2 + [Y_MSG] * 2, owner, place, d_gate_up, x_band)
    x1, x3, y1, y3 = swap(x1, "x", 1), swap(x3, "x", 3), swap(y1, "y", 1), swap(y3, "y", 3)
    (own,) = packed(pack_own_kernel, "pack_own", [OWN_MSG], owner, place, d_gate_up)
    f0, f1 = swap(x1[:, X_FWD], "x", 3), swap(x3[:, X_FWD], "x", 1)
    f2, f3 = swap(y1[:, Y_FWD], "y", 3), swap(y3[:, Y_FWD], "y", 1)
    pieces = (own, x_band, x1, x3, y1, y3, f0, f1, f2, f3)
    wide, tall = partials(1, pieces)
    far_wide, far_tall = swap(wide, "core", 1), swap(tall, "core", 1)
    wide, tall = partials(0, pieces)
    py0, py1, py2, py3, px0, px1, px2, px3 = chip_sum(place, wide, tall, far_wide, far_tall)
    ry2, rx2 = swap(py2, "y", 2), swap(px2, "x", 2)
    ry1, rx1 = swap(py1, "y", 1), swap(px1, "x", 1)
    ry3, rx3 = swap(py3, "y", 3), swap(px3, "x", 3)
    message = ring_sum((py0, ry1, ry2, ry3, px0, rx1, rx2, rx3))
    message, statistics = lax.optimization_barrier((message, statistics))
    message = lax.all_to_all(message, ("z_hi", "z_lo"), 0, 0, tiled=True)
    main, spread = line_sum(message.reshape(8, PIECE, B))

    far = swap(main, "z_lo", 1)
    spread = lax.all_to_all(spread, ("z_hi", "x", "core", "z_lo"), 0, 0, tiled=True)
    both = choose(owner, place, main, far, spread)
    r2, r1, r3 = swap(both, "y", 2), swap(both, "y", 1), swap(both, "y", 3)
    directions, left_new, right_new = roots(place, (both, r1, r2, r3), statistics, stat_left[0], stat_right[0])
    a2, a1, a3 = swap(directions, "z_hi", 2), swap(directions, "z_hi", 1), swap(directions, "z_hi", 3)
    plane = jnp.concatenate([directions, a1, a2, a3])
    b2, b1, b3 = swap(plane, "x", 2), swap(plane, "x", 1), swap(plane, "x", 3)
    near = (plane, b1, b2, b3)
    across = tuple(swap(v, "core", 1) for v in near)
    out = put_blocks(owner, place, near + across, bucket)
    return (out, left_new[None], right_new[None])


def solution(mesh):
    fine = Mesh(np.asarray(mesh.devices).reshape(FINE_SIZES), FINE)
    dp, node = FINE[:3], FINE[3:]
    placed = (P(dp + node, None), P(dp + node, None), P(), P(dp, None, node, None), P(dp, None, node, None))
    return jax.shard_map(
        shards,
        mesh=fine,
        in_specs=placed,
        out_specs=(P(node, None), P(dp, None, node, None), P(dp, None, node, None)),
        check_vma=False,
    )
```

time: 321 us -> 230 us (0.72)
  Pallas kernels: 88.6 us -> 17.2 us
  blocking collectives: 0 us -> 26.1 us
  waiting for transfers between devices: 131 us -> 112 us
  starting transfers between devices: 70.3 us -> 55 us
  local copies, waits for them, and re-layouts: 10.9 us -> 3.37 us
    pallas_call x2 -> x7, Pallas kernels: 78.5 us -> 7.95 us  [the longest x2 3.14 us: packed(): pl.pallas_call(kernel, out_shape=[jax.ShapeDtypeStruct((rows, w), jnp.bfl...]
    all_to_all x2 -> x1, waiting for transfers between devices: 30.5 us -> 3.16 us  [shards(): lax.all_to_all(spread, ('z_hi', 'x', 'core', 'z_lo'), 0, 0, tiled=True)]
    all_to_all x0 -> x1, blocking collectives: none -> 26.1 us  [shards(): message = lax.all_to_all(message, ('z_hi', 'z_lo'), 0, 0, tiled=True)]
    ppermute x29 -> x30, waiting for transfers between devices: 85.4 us -> 108 us  [swap(): return lax.ppermute(value, axis, [(i, i ^ mask) for i in range(size)])]
    ppermute x4 -> x0, waiting for transfers between devices: 15.2 us -> none  [the longest x2 11 us: swap_core(): return lax.ppermute(value, ('core', 'y'), pairs)]
    all_to_all x2 -> x1, starting transfers between devices: 15 us -> 8.07 us  [shards(): lax.all_to_all(spread, ('z_hi', 'x', 'core', 'z_lo'), 0, 0, tiled=True)]
    ppermute x4 -> x0, starting transfers between devices: 6.78 us -> none  [the longest x2 3.6 us: swap_core(): return lax.ppermute(value, ('x', 'core'), pairs)]
    slice x10 -> x4, local copies, waits for them, and re-layouts: 3.91 us -> 0.1 us  [the longest x2 0.05 us: shards(): f0, f1 = (swap(x1[:, X_FWD], 'x', 3), swap(x3[:, X_FWD], 'x', 1))]
  transfers between devices with their start and end apart: 37 -> 32, of which waited for: 21 -> 18; matrix products, arithmetic and copies ran while one was open for 2% -> 0% of each run, Pallas kernels for 2% -> 3%
where the time goes in v2:
time: 230 us; the launch traced here: 229 us
  waiting for transfers between devices  112 us (49%)
  starting transfers between devices  55 us (24%)
  blocking collectives  26.1 us (11%)
  Pallas kernels  17.2 us (7%)
  between operations  14.3 us (6%)
  local copies, waits for them, and re-layouts  3.37 us (1%)
    ppermute x30, waiting for transfers between devices, swap(): return lax.ppermute(value, axis, [(i, i ^ mask) for i in range(size)])  108 us
    ppermute x30, starting transfers between devices, swap(): return lax.ppermute(value, axis, [(i, i ^ mask) for i in range(size)])  46.9 us
    all_to_all x1, blocking collectives, shards(): message = lax.all_to_all(message, ('z_hi', 'z_lo'), 0, 0, tiled=True)  26.1 us
    all_to_all x1, starting transfers between devices, shards(): lax.all_to_all(spread, ('z_hi', 'x', 'core', 'z_lo'), 0, 0, tiled=True)  8.07 us
    pallas_call x1, Pallas kernels, roots(): pl.pallas_call(root_kernel, out_shape=[jax.ShapeDtypeStruct((SLOTS * 64,...  7 us
  transfers between devices with their start and end apart: 32, of which 18 were waited for; matrix products, arithmetic and copies ran while one was open for 0% of the time, Pallas kernels for 3%

profile of v2, /device:TPU:1, one launch (start us, length us, event | category | flops | bytes accessed | tf_op | source)
XLA Modules:
  0.0 229.4 jit_solution(6165301262781744164)
XLA Ops:
  7.2 1.1 bitcast_convert_fusion
  9.2 2.3 %copy-done = bf16[128,18432]{1,0:T(8,128)(2,1)S(1)} copy-done((bf16[128,18432]{1,0:T(8,128)(2,1)S(1)}, bf16[128,18432]{1,0:T(8,128)(2,1)}, u32[]{:S(2)}) %copy-start) | copy-done | bytes 4718616
  11.5 2.1 pack.1
  13.6 2.1 collective-permute-start
  15.7 1.8 collective-permute-start.1
  17.5 1.3 collective-permute-start.2
  18.8 1.9 collective-permute-start.3
  20.7 17.9 %collective-permute-done.x1 = bf16[128,4352]{1,0:T(8,128)(2,1)S(1)} collective-permute-done((bf16[128,4352]{1,0:T(8,128)(2,1)S(1)}, bf16[128,4352]{1,0:T(8,128)(2,1)S(1)}, u32[]{:S(2)}, u32[]{:S(2)}) %collective-permute-start) | collective-permute-done | bytes 1114144 | tf_op jit(solution)/shard_map/ppermute | solution.py:35
  38.7 3.9 %collective-permute-start.4 = (bf16[128,1536]{1,0:T(8,128)(2,1)S(1)}, bf16[128,1536]{1,0:T(8,128)(2,1)S(1)}, u32[]{:S(2)}, u32[]{:S(2)}) collective-permute-start(bf16[128,1536]{1,0:T(8,128)(2,1)S(1)} %slice.16), channel_id=1, source_target_pairs={{0,48},{16,32},{32,16},{48,0},{1,49},{17,33},{33,17},{49,1},{2,50}... | collective-permute-start | bytes 1179656 | tf_op jit(solution)/shard_map/ppermute | solution.py:35
  42.8 4.9 %collective-permute-done.2.y1 = bf16[128,3584]{1,0:T(8,128)(2,1)S(1)} collective-permute-done((bf16[128,3584]{1,0:T(8,128)(2,1)S(1)}, bf16[128,3584]{1,0:T(8,128)(2,1)S(1)}, u32[]{:S(2)}, u32[]{:S(2)}) %collective-permute-start.2) | collective-permute-done | bytes 917536 | tf_op jit(solution)/shard_map/ppermute | solution.py:35
  47.6 4.1 %collective-permute-start.6 = (bf16[128,1280]{1,0:T(8,128)(2,1)S(1)}, bf16[128,1280]{1,0:T(8,128)(2,1)S(1)}, u32[]{:S(2)}, u32[]{:S(2)}) collective-permute-start(bf16[128,1280]{1,0:T(8,128)(2,1)S(1)} %slice.18), channel_id=1, source_target_pairs={{0,6},{2,4},{4,2},{6,0},{1,7},{3,5},{5,3},{7,1},{8,14},{10,12},{12... | collective-permute-start | bytes 983048 | tf_op jit(solution)/shard_map/ppermute | solution.py:35
  51.9 1.1 pack_own.1.own
  52.9 14.3 %collective-permute-done.6.f2 = bf16[128,1280]{1,0:T(8,128)(2,1)S(1)} collective-permute-done((bf16[128,1280]{1,0:T(8,128)(2,1)S(1)}, bf16[128,1280]{1,0:T(8,128)(2,1)S(1)}, u32[]{:S(2)}, u32[]{:S(2)}) %collective-permute-start.6) | collective-permute-done | bytes 327712 | tf_op jit(solution)/shard_map/ppermute | solution.py:35
  67.3 1.5 partials.3
  68.7 2.3 %collective-permute-start.8 = (bf16[512,1280]{1,0:T(8,128)(2,1)S(1)}, bf16[512,1280]{1,0:T(8,128)(2,1)S(1)}, u32[]{:S(2)}, u32[]{:S(2)}) collective-permute-start(bf16[512,1280]{1,0:T(8,128)(2,1)S(1)} %get-tuple-element.32), channel_id=1, source_target_pairs={{0,8},{8,0},{1,9},{9,1},{2,10},{10,2},{3,11},{11,3},{4,12},{12,4},... | collective-permute-start | bytes 3932168 | tf_op jit(solution)/shard_map/ppermute | solution.py:35
  71.2 1.5 partials.2
  72.6 2.6 %collective-permute-done.9.far_tall = bf16[512,1024]{1,0:T(8,128)(2,1)S(1)} collective-permute-done((bf16[512,1024]{1,0:T(8,128)(2,1)S(1)}, bf16[512,1024]{1,0:T(8,128)(2,1)S(1)}, u32[]{:S(2)}, u32[]{:S(2)}) %collective-permute-start.9) | collective-permute-done | bytes 1048608 | tf_op jit(solution)/shard_map/ppermute | solution.py:35
  75.2 1.2 chip_sum.1
  76.6 2.3 collective-permute-start.11
  78.9 1.6 collective-permute-start.12
  81.1 3.0 %collective-permute-done.13.rx1 = bf16[512,256]{1,0:T(8,128)(2,1)S(1)} collective-permute-done((bf16[512,256]{1,0:T(8,128)(2,1)S(1)}, bf16[512,256]{1,0:T(8,128)(2,1)S(1)}, u32[]{:S(2)}, u32[]{:S(2)}) %collective-permute-start.13) | collective-permute-done | bytes 262176 | tf_op jit(solution)/shard_map/ppermute | solution.py:35
  84.2 4.3 %collective-permute-done.14.rx2 = bf16[512,256]{1,0:T(8,128)(2,1)S(1)} collective-permute-done((bf16[512,256]{1,0:T(8,128)(2,1)S(1)}, bf16[512,256]{1,0:T(8,128)(2,1)S(1)}, u32[]{:S(2)}, u32[]{:S(2)}) %collective-permute-start.14) | collective-permute-done | bytes 262176 | tf_op jit(solution)/shard_map/ppermute | solution.py:35
  88.5 7.2 %collective-permute-done.15.rx3 = bf16[512,256]{1,0:T(8,128)(2,1)S(1)} collective-permute-done((bf16[512,256]{1,0:T(8,128)(2,1)S(1)}, bf16[512,256]{1,0:T(8,128)(2,1)S(1)}, u32[]{:S(2)}, u32[]{:S(2)}) %collective-permute-start.15) | collective-permute-done | bytes 262176 | tf_op jit(solution)/shard_map/ppermute | solution.py:35
  96.1 26.1 %all_to_all.20.arrived = bf16[8,80,512]{2,1,0:T(8,128)(2,1)S(1)} all-to-all(bf16[8,80,512]{2,1,0:T(8,128)(2,1)S(1)} %bitcast.14), channel_id=1, replica_groups=mesh['z_hi'=4,'x'=4,'core'=2,'y'=4,'z_lo'=2] {'z_hi','z_lo'}, dimensions={0} | all-to-all | bytes 1310720 | tf_op jit(solution)/shard_map/all_to_all | solution.py:436
  123.1 8.1 %all-to-all-start.1 = ((bf16[64,16,256]{2,1,0:T(8,128)(2,1)}), bf16[64,16,256]{2,1,0:T(8,128)(2,1)S(1)}, u32[]{:S(2)}, u32[]{:S(2)}) async-start(bf16[64,16,256]{2,1,0:T(8,128)(2,1)} %bitcast.18), calls=%async_computation.1 | async-start | bytes 1048576 | tf_op jit(solution)/shard_map/all_to_all | solution.py:440
  131.2 1.5 collective-permute-start.16
  132.7 13.2 %collective-permute-done.16.far = bf16[64,512]{1,0:T(8,128)(2,1)S(1)} collective-permute-done((bf16[64,512]{1,0:T(8,128)(2,1)S(1)}, bf16[64,512]{1,0:T(8,128)(2,1)S(1)}, u32[]{:S(2)}, u32[]{:S(2)}) %collective-permute-start.16) | collective-permute-done | bytes 65568 | tf_op jit(solution)/shard_map/ppermute | solution.py:35
  145.8 3.2 %all-to-all-done.1 = bf16[64,16,256]{2,1,0:T(8,128)(2,1)S(1)} async-done(((bf16[64,16,256]{2,1,0:T(8,128)(2,1)}), bf16[64,16,256]{2,1,0:T(8,128)(2,1)S(1)}, u32[]{:S(2)}, u32[]{:S(2)}) %all-to-all-start.1) | async-done | bytes 524320 | tf_op jit(solution)/shard_map/all_to_all | solution.py:440
  149.7 3.0 %collective-permute-start.18 = (bf16[256,512]{1,0:T(8,128)(2,1)S(1)}, bf16[256,512]{1,0:T(8,128)(2,1)S(1)}, u32[]{:S(2)}, u32[]{:S(2)}) collective-permute-start(bf16[256,512]{1,0:T(8,128)(2,1)S(1)} %choose.1.r0), channel_id=1, source_target_pairs={{0,4},{2,6},{4,0},{6,2},{1,5},{3,7},{5,1},{7,3},{8,12},{10,14},{12... | collective-permute-start | bytes 786440 | tf_op jit(solution)/shard_map/ppermute | solution.py:35
  153.6 3.2 %collective-permute-done.17.r1 = bf16[256,512]{1,0:T(8,128)(2,1)S(1)} collective-permute-done((bf16[256,512]{1,0:T(8,128)(2,1)S(1)}, bf16[256,512]{1,0:T(8,128)(2,1)S(1)}, u32[]{:S(2)}, u32[]{:S(2)}) %collective-permute-start.17) | collective-permute-done | bytes 262176 | tf_op jit(solution)/shard_map/ppermute | solution.py:35
  156.8 7.0 %collective-permute-done.18.r2 = bf16[256,512]{1,0:T(8,128)(2,1)S(1)} collective-permute-done((bf16[256,512]{1,0:T(8,128)(2,1)S(1)}, bf16[256,512]{1,0:T(8,128)(2,1)S(1)}, u32[]{:S(2)}, u32[]{:S(2)}) %collective-permute-start.18) | collective-permute-done | bytes 262176 | tf_op jit(solution)/shard_map/ppermute | solution.py:35
  163.8 2.3 collective-permute-done.19.r3
  166.1 7.0 %roots.1 = (bf16[128,512]{1,0:T(8,128)(2,1)S(1)}, f32[2,64,512]{2,1,0:T(8,128)}, f32[2,64,512]{2,1,0:T(8,128)}) custom-call(s32[5]{0:T(128)S(1)} %stack.23.place, bf16[256,512]{1,0:T(8,128)(2,1)S(1)} %choose.1.r0, bf16[256,512]{1,0:T(8,128)(2,1)S(1)} %collective-permute-done.17.r1, bf16[256,512]{1,0:T(8,128)(2,1)S(1)} %collective-permute-done.18.r2, ...), custom_call_target="tpu_custom_call" | custom-call | tf_op jit(solution)/shard_map/roots/pallas_call | solution.py:359
  173.1 2.0 collective-permute-start.20
  175.1 2.3 collective-permute-start.21
  177.4 1.6 collective-permute-start.22
  178.9 6.2 %collective-permute-done.20 = bf16[128,512]{1,0:T(8,128)(2,1)S(1)} collective-permute-done((bf16[128,512]{1,0:T(8,128)(2,1)S(1)}, bf16[128,512]{1,0:T(8,128)(2,1)S(1)}, u32[]{:S(2)}, u32[]{:S(2)}) %collective-permute-start.20) | collective-permute-done | bytes 131104 | tf_op jit(solution)/shard_map/ppermute | solution.py:35
  185.2 4.1 %collective-permute-done.22 = bf16[128,512]{1,0:T(8,128)(2,1)S(1)} collective-permute-done((bf16[128,512]{1,0:T(8,128)(2,1)S(1)}, bf16[128,512]{1,0:T(8,128)(2,1)S(1)}, u32[]{:S(2)}, u32[]{:S(2)}) %collective-permute-start.22) | collective-permute-done | bytes 131104 | tf_op jit(solution)/shard_map/ppermute | solution.py:35
  189.6 2.7 %collective-permute-start.24 = (bf16[512,512]{1,0:T(8,128)(2,1)S(1)}, bf16[512,512]{1,0:T(8,128)(2,1)S(1)}, u32[]{:S(2)}, u32[]{:S(2)}) collective-permute-start(bf16[512,512]{1,0:T(8,128)(2,1)S(1)} %constant_dynamic-update-slice_fusion.refs_0_), channel_id=1, source_target_pairs={{0,32},{16,48},{32,0},{48,16},{1,33},{17,49},{33,1},{49,17},{2,34}... | collective-permute-start | bytes 1572872 | tf_op jit(solution)/shard_map/ppermute | solution.py:35
  192.3 1.0 collective-permute-start.25
  193.3 1.7 collective-permute-start.26
  195.0 6.9 %collective-permute-done.23.refs_1_ = bf16[512,512]{1,0:T(8,128)(2,1)S(1)} collective-permute-done((bf16[512,512]{1,0:T(8,128)(2,1)S(1)}, bf16[512,512]{1,0:T(8,128)(2,1)S(1)}, u32[]{:S(2)}, u32[]{:S(2)}) %collective-permute-start.23) | collective-permute-done | bytes 524320 | tf_op jit(solution)/shard_map/ppermute | solution.py:35
  201.9 3.2 %collective-permute-start.27 = (bf16[512,512]{1,0:T(8,128)(2,1)S(1)}, bf16[512,512]{1,0:T(8,128)(2,1)S(1)}, u32[]{:S(2)}, u32[]{:S(2)}) collective-permute-start(bf16[512,512]{1,0:T(8,128)(2,1)S(1)} %collective-permute-done.23.refs_1_), channel_id=1, source_target_pairs={{0,8},{8,0},{1,9},{9,1},{2,10},{10,2},{3,11},{11,3},{4,12},{12,4},... | collective-permute-start | bytes 1572872 | tf_op jit(solution)/shard_map/ppermute | solution.py:35
  205.1 9.5 %collective-permute-done.24.refs_2_ = bf16[512,512]{1,0:T(8,128)(2,1)S(1)} collective-permute-done((bf16[512,512]{1,0:T(8,128)(2,1)S(1)}, bf16[512,512]{1,0:T(8,128)(2,1)S(1)}, u32[]{:S(2)}, u32[]{:S(2)}) %collective-permute-start.24) | collective-permute-done | bytes 524320 | tf_op jit(solution)/shard_map/ppermute | solution.py:35
  214.7 1.8 collective-permute-start.28
  216.7 2.3 %collective-permute-start.29 = (bf16[512,512]{1,0:T(8,128)(2,1)S(1)}, bf16[512,512]{1,0:T(8,128)(2,1)S(1)}, u32[]{:S(2)}, u32[]{:S(2)}) collective-permute-start(bf16[512,512]{1,0:T(8,128)(2,1)S(1)} %collective-permute-done.25.refs_3_), channel_id=1, source_target_pairs={{0,8},{8,0},{1,9},{9,1},{2,10},{10,2},{3,11},{11,3},{4,12},{12,4},... | collective-permute-start | bytes 1572872 | tf_op jit(solution)/shard_map/ppermute | solution.py:35
  219.1 1.5 collective-permute-done.29.refs_7_
  220.6 2.0 put_blocks.1
  (53 shorter events, 5.6 us)
Async XLA Ops:
  7.2 2.0 copy-start.2
  7.2 2.0 copy-start.6
  7.2 88.9 %all-gather.2.cloned.1.call-start = ((), (), s32[]{:S(2)}) async-start(), calls=%async_computation.2 | async-start | bytes 2359296 | tf_op jit(solution)/shard_map/all_gather | solution.py:419
  9.2 2.3 %copy-start = (bf16[128,18432]{1,0:T(8,128)(2,1)S(1)}, bf16[128,18432]{1,0:T(8,128)(2,1)}, u32[]{:S(2)}) copy-start(bf16[128,18432]{1,0:T(8,128)(2,1)} %d.3) | copy-start | bytes 14155780
  13.6 25.1 %collective-permute-start = (bf16[128,4352]{1,0:T(8,128)(2,1)S(1)}, bf16[128,4352]{1,0:T(8,128)(2,1)S(1)}, u32[]{:S(2)}, u32[]{:S(2)}) collective-permute-start(bf16[128,4352]{1,0:T(8,128)(2,1)S(1)} %get-tuple-element.26), channel_id=1, source_target_pairs={{0,16},{16,0},{32,48},{48,32},{1,17},{17,1},{33,49},{49,33},{2,18}... | collective-permute-start | bytes 3342344 | tf_op jit(solution)/shard_map/ppermute | solution.py:35
  15.7 26.9 %collective-permute-start.1 = (bf16[128,4352]{1,0:T(8,128)(2,1)S(1)}, bf16[128,4352]{1,0:T(8,128)(2,1)S(1)}, u32[]{:S(2)}, u32[]{:S(2)}) collective-permute-start(bf16[128,4352]{1,0:T(8,128)(2,1)S(1)} %get-tuple-element.27), channel_id=1, source_target_pairs={{0,48},{16,32},{32,16},{48,0},{1,49},{17,33},{33,17},{49,1},{2,50}... | collective-permute-start | bytes 3342344 | tf_op jit(solution)/shard_map/ppermute | solution.py:35
  17.5 30.1 %collective-permute-start.2 = (bf16[128,3584]{1,0:T(8,128)(2,1)S(1)}, bf16[128,3584]{1,0:T(8,128)(2,1)S(1)}, u32[]{:S(2)}, u32[]{:S(2)}) collective-permute-start(bf16[128,3584]{1,0:T(8,128)(2,1)S(1)} %get-tuple-element.28), channel_id=1, source_target_pairs={{0,2},{2,0},{4,6},{6,4},{1,3},{3,1},{5,7},{7,5},{8,10},{10,8},{12,... | collective-permute-start | bytes 2752520 | tf_op jit(solution)/shard_map/ppermute | solution.py:35
  18.8 32.9 %collective-permute-start.3 = (bf16[128,3584]{1,0:T(8,128)(2,1)S(1)}, bf16[128,3584]{1,0:T(8,128)(2,1)S(1)}, u32[]{:S(2)}, u32[]{:S(2)}) collective-permute-start(bf16[128,3584]{1,0:T(8,128)(2,1)S(1)} %get-tuple-element.29), channel_id=1, source_target_pairs={{0,6},{2,4},{4,2},{6,0},{1,7},{3,5},{5,3},{7,1},{8,14},{10,12},{12... | collective-permute-start | bytes 2752520 | tf_op jit(solution)/shard_map/ppermute | solution.py:35
  38.7 28.6 %collective-permute-start.4 = (bf16[128,1536]{1,0:T(8,128)(2,1)S(1)}, bf16[128,1536]{1,0:T(8,128)(2,1)S(1)}, u32[]{:S(2)}, u32[]{:S(2)}) collective-permute-start(bf16[128,1536]{1,0:T(8,128)(2,1)S(1)} %slice.16), channel_id=1, source_target_pairs={{0,48},{16,32},{32,16},{48,0},{1,49},{17,33},{33,17},{49,1},{2,50}... | collective-permute-start | bytes 1179656 | tf_op jit(solution)/shard_map/ppermute | solution.py:35
  42.7 24.6 %collective-permute-start.5 = (bf16[128,1536]{1,0:T(8,128)(2,1)S(1)}, bf16[128,1536]{1,0:T(8,128)(2,1)S(1)}, u32[]{:S(2)}, u32[]{:S(2)}) collective-permute-start(bf16[128,1536]{1,0:T(8,128)(2,1)S(1)} %slice.17), channel_id=1, source_target_pairs={{0,16},{16,0},{32,48},{48,32},{1,17},{17,1},{33,49},{49,33},{2,18}... | collective-permute-start | bytes 1179656 | tf_op jit(solution)/shard_map/ppermute | solution.py:35
  47.6 19.6 %collective-permute-start.6 = (bf16[128,1280]{1,0:T(8,128)(2,1)S(1)}, bf16[128,1280]{1,0:T(8,128)(2,1)S(1)}, u32[]{:S(2)}, u32[]{:S(2)}) collective-permute-start(bf16[128,1280]{1,0:T(8,128)(2,1)S(1)} %slice.18), channel_id=1, source_target_pairs={{0,6},{2,4},{4,2},{6,0},{1,7},{3,5},{5,3},{7,1},{8,14},{10,12},{12... | collective-permute-start | bytes 983048 | tf_op jit(solution)/shard_map/ppermute | solution.py:35
  51.8 15.5 %collective-permute-start.7 = (bf16[128,1280]{1,0:T(8,128)(2,1)S(1)}, bf16[128,1280]{1,0:T(8,128)(2,1)S(1)}, u32[]{:S(2)}, u32[]{:S(2)}) collective-permute-start(bf16[128,1280]{1,0:T(8,128)(2,1)S(1)} %slice.19), channel_id=1, source_target_pairs={{0,2},{2,0},{4,6},{6,4},{1,3},{3,1},{5,7},{7,5},{8,10},{10,8},{12,... | collective-permute-start | bytes 983048 | tf_op jit(solution)/shard_map/ppermute | solution.py:35
  68.7 6.5 %collective-permute-start.8 = (bf16[512,1280]{1,0:T(8,128)(2,1)S(1)}, bf16[512,1280]{1,0:T(8,128)(2,1)S(1)}, u32[]{:S(2)}, u32[]{:S(2)}) collective-permute-start(bf16[512,1280]{1,0:T(8,128)(2,1)S(1)} %get-tuple-element.32), channel_id=1, source_target_pairs={{0,8},{8,0},{1,9},{9,1},{2,10},{10,2},{3,11},{11,3},{4,12},{12,4},... | collective-permute-start | bytes 3932168 | tf_op jit(solution)/shard_map/ppermute | solution.py:35
  71.1 4.2 %collective-permute-start.9 = (bf16[512,1024]{1,0:T(8,128)(2,1)S(1)}, bf16[512,1024]{1,0:T(8,128)(2,1)S(1)}, u32[]{:S(2)}, u32[]{:S(2)}) collective-permute-start(bf16[512,1024]{1,0:T(8,128)(2,1)S(1)} %get-tuple-element.33), channel_id=1, source_target_pairs={{0,8},{8,0},{1,9},{9,1},{2,10},{10,2},{3,11},{11,3},{4,12},{12,4},... | collective-permute-start | bytes 3145736 | tf_op jit(solution)/shard_map/ppermute | solution.py:35
  76.4 7.6 %collective-permute-start.13 = (bf16[512,256]{1,0:T(8,128)(2,1)S(1)}, bf16[512,256]{1,0:T(8,128)(2,1)S(1)}, u32[]{:S(2)}, u32[]{:S(2)}) collective-permute-start(bf16[512,256]{1,0:T(8,128)(2,1)S(1)} %get-tuple-element.39), channel_id=1, source_target_pairs={{0,16},{16,0},{32,48},{48,32},{1,17},{17,1},{33,49},{49,33},{2,18}... | collective-permute-start | bytes 786440 | tf_op jit(solution)/shard_map/ppermute | solution.py:35
  76.5 19.3 %collective-permute-start.10 = (bf16[128,1280]{1,0:T(8,128)(2,1)S(1)}, bf16[128,1280]{1,0:T(8,128)(2,1)S(1)}, u32[]{:S(2)}, u32[]{:S(2)}) collective-permute-start(bf16[128,1280]{1,0:T(8,128)(2,1)S(1)} %get-tuple-element.35), channel_id=1, source_target_pairs={{0,2},{2,0},{4,6},{6,4},{1,3},{3,1},{5,7},{7,5},{8,10},{10,8},{12,... | collective-permute-start | bytes 983048 | tf_op jit(solution)/shard_map/ppermute | solution.py:35
  76.6 19.2 %collective-permute-start.11 = (bf16[128,1280]{1,0:T(8,128)(2,1)S(1)}, bf16[128,1280]{1,0:T(8,128)(2,1)S(1)}, u32[]{:S(2)}, u32[]{:S(2)}) collective-permute-start(bf16[128,1280]{1,0:T(8,128)(2,1)S(1)} %get-tuple-element.36), channel_id=1, source_target_pairs={{0,4},{2,6},{4,0},{6,2},{1,5},{3,7},{5,1},{7,3},{8,12},{10,14},{12... | collective-permute-start | bytes 983048 | tf_op jit(solution)/shard_map/ppermute | solution.py:35
  78.9 16.9 %collective-permute-start.12 = (bf16[128,1280]{1,0:T(8,128)(2,1)S(1)}, bf16[128,1280]{1,0:T(8,128)(2,1)S(1)}, u32[]{:S(2)}, u32[]{:S(2)}) collective-permute-start(bf16[128,1280]{1,0:T(8,128)(2,1)S(1)} %get-tuple-element.37), channel_id=1, source_target_pairs={{0,6},{2,4},{4,2},{6,0},{1,7},{3,5},{5,3},{7,1},{8,14},{10,12},{12... | collective-permute-start | bytes 983048 | tf_op jit(solution)/shard_map/ppermute | solution.py:35
  80.5 8.1 %collective-permute-start.14 = (bf16[512,256]{1,0:T(8,128)(2,1)S(1)}, bf16[512,256]{1,0:T(8,128)(2,1)S(1)}, u32[]{:S(2)}, u32[]{:S(2)}) collective-permute-start(bf16[512,256]{1,0:T(8,128)(2,1)S(1)} %get-tuple-element.40), channel_id=1, source_target_pairs={{0,32},{16,48},{32,0},{48,16},{1,33},{17,49},{33,1},{49,17},{2,34}... | collective-permute-start | bytes 786440 | tf_op jit(solution)/shard_map/ppermute | solution.py:35
  84.0 11.8 %collective-permute-start.15 = (bf16[512,256]{1,0:T(8,128)(2,1)S(1)}, bf16[512,256]{1,0:T(8,128)(2,1)S(1)}, u32[]{:S(2)}, u32[]{:S(2)}) collective-permute-start(bf16[512,256]{1,0:T(8,128)(2,1)S(1)} %get-tuple-element.41), channel_id=1, source_target_pairs={{0,48},{16,32},{32,16},{48,0},{1,49},{17,33},{33,17},{49,1},{2,50}... | collective-permute-start | bytes 786440 | tf_op jit(solution)/shard_map/ppermute | solution.py:35
  122.2 43.9 %copy-start.1 = (bf16[4,512,512]{2,1,0:T(8,128)(2,1)S(1)}, bf16[4,512,512]{2,1,0:T(8,128)(2,1)}, u32[]{:S(2)}) copy-start(bf16[4,512,512]{2,1,0:T(8,128)(2,1)} %all-gather.2.cloned.1.call-done.statistics) | copy-start | bytes 6291460
  122.2 43.9 %copy-start.3 = (f32[1,2,64,512]{3,2,1,0:T(8,128)S(1)}, f32[1,2,64,512]{3,2,1,0:T(8,128)}, u32[]{:S(2)}) copy-start(f32[1,2,64,512]{3,2,1,0:T(8,128)} %param.9) | copy-start | bytes 786436
  122.2 43.9 %copy-start.4 = (f32[1,2,64,512]{3,2,1,0:T(8,128)S(1)}, f32[1,2,64,512]{3,2,1,0:T(8,128)}, u32[]{:S(2)}) copy-start(f32[1,2,64,512]{3,2,1,0:T(8,128)} %param.8) | copy-start | bytes 786436
  122.3 0.8 copy-start.5
  123.1 25.9 %all-to-all-start.1 = ((bf16[64,16,256]{2,1,0:T(8,128)(2,1)}), bf16[64,16,256]{2,1,0:T(8,128)(2,1)S(1)}, u32[]{:S(2)}, u32[]{:S(2)}) async-start(bf16[64,16,256]{2,1,0:T(8,128)(2,1)} %bitcast.18), calls=%async_computation.1 | async-start | bytes 1048576 | tf_op jit(solution)/shard_map/all_to_all | solution.py:440
  131.2 14.6 %collective-permute-start.16 = (bf16[64,512]{1,0:T(8,128)(2,1)S(1)}, bf16[64,512]{1,0:T(8,128)(2,1)S(1)}, u32[]{:S(2)}, u32[]{:S(2)}) collective-permute-start(bf16[64,512]{1,0:T(8,128)(2,1)S(1)} %get-tuple-element.43.main), channel_id=1, source_target_pairs={{0,1},{1,0},{2,3},{3,2},{4,5},{5,4},{6,7},{7,6},{8,9},{9,8},{10,11... | collective-permute-start | bytes 196616 | tf_op jit(solution)/shard_map/ppermute | solution.py:35
  149.6 7.2 %collective-permute-start.17 = (bf16[256,512]{1,0:T(8,128)(2,1)S(1)}, bf16[256,512]{1,0:T(8,128)(2,1)S(1)}, u32[]{:S(2)}, u32[]{:S(2)}) collective-permute-start(bf16[256,512]{1,0:T(8,128)(2,1)S(1)} %choose.1.r0), channel_id=1, source_target_pairs={{0,2},{2,0},{4,6},{6,4},{1,3},{3,1},{5,7},{7,5},{8,10},{10,8},{12,... | collective-permute-start | bytes 786440 | tf_op jit(solution)/shard_map/ppermute | solution.py:35
  149.7 14.1 %collective-permute-start.18 = (bf16[256,512]{1,0:T(8,128)(2,1)S(1)}, bf16[256,512]{1,0:T(8,128)(2,1)S(1)}, u32[]{:S(2)}, u32[]{:S(2)}) collective-permute-start(bf16[256,512]{1,0:T(8,128)(2,1)S(1)} %choose.1.r0), channel_id=1, source_target_pairs={{0,4},{2,6},{4,0},{6,2},{1,5},{3,7},{5,1},{7,3},{8,12},{10,14},{12... | collective-permute-start | bytes 786440 | tf_op jit(solution)/shard_map/ppermute | solution.py:35
  152.7 13.4 %collective-permute-start.19 = (bf16[256,512]{1,0:T(8,128)(2,1)S(1)}, bf16[256,512]{1,0:T(8,128)(2,1)S(1)}, u32[]{:S(2)}, u32[]{:S(2)}) collective-permute-start(bf16[256,512]{1,0:T(8,128)(2,1)S(1)} %choose.1.r0), channel_id=1, source_target_pairs={{0,6},{2,4},{4,2},{6,0},{1,7},{3,5},{5,3},{7,1},{8,14},{10,12},{12... | collective-permute-start | bytes 786440 | tf_op jit(solution)/shard_map/ppermute | solution.py:35
  173.1 12.1 %collective-permute-start.20 = (bf16[128,512]{1,0:T(8,128)(2,1)S(1)}, bf16[128,512]{1,0:T(8,128)(2,1)S(1)}, u32[]{:S(2)}, u32[]{:S(2)}) collective-permute-start(bf16[128,512]{1,0:T(8,128)(2,1)S(1)} %get-tuple-element.46), channel_id=1, source_target_pairs={{0,64},{64,0},{128,192},{192,128},{1,65},{65,1},{129,193},{193,129... | collective-permute-start | bytes 393224 | tf_op jit(solution)/shard_map/ppermute | solution.py:35
  175.1 10.1 %collective-permute-start.21 = (bf16[128,512]{1,0:T(8,128)(2,1)S(1)}, bf16[128,512]{1,0:T(8,128)(2,1)S(1)}, u32[]{:S(2)}, u32[]{:S(2)}) collective-permute-start(bf16[128,512]{1,0:T(8,128)(2,1)S(1)} %get-tuple-element.46), channel_id=1, source_target_pairs={{0,128},{64,192},{128,0},{192,64},{1,129},{65,193},{129,1},{193,65... | collective-permute-start | bytes 393224 | tf_op jit(solution)/shard_map/ppermute | solution.py:35
  177.4 11.9 %collective-permute-start.22 = (bf16[128,512]{1,0:T(8,128)(2,1)S(1)}, bf16[128,512]{1,0:T(8,128)(2,1)S(1)}, u32[]{:S(2)}, u32[]{:S(2)}) collective-permute-start(bf16[128,512]{1,0:T(8,128)(2,1)S(1)} %get-tuple-element.46), channel_id=1, source_target_pairs={{0,192},{64,128},{128,64},{192,0},{1,193},{65,129},{129,65},{193,1... | collective-permute-start | bytes 393224 | tf_op jit(solution)/shard_map/ppermute | solution.py:35
  189.3 12.6 %collective-permute-start.23 = (bf16[512,512]{1,0:T(8,128)(2,1)S(1)}, bf16[512,512]{1,0:T(8,128)(2,1)S(1)}, u32[]{:S(2)}, u32[]{:S(2)}) collective-permute-start(bf16[512,512]{1,0:T(8,128)(2,1)S(1)} %constant_dynamic-update-slice_fusion.refs_0_), channel_id=1, source_target_pairs={{0,16},{16,0},{32,48},{48,32},{1,17},{17,1},{33,49},{49,33},{2,18}... | collective-permute-start | bytes 1572872 | tf_op jit(solution)/shard_map/ppermute | solution.py:35
  189.6 25.1 %collective-permute-start.24 = (bf16[512,512]{1,0:T(8,128)(2,1)S(1)}, bf16[512,512]{1,0:T(8,128)(2,1)S(1)}, u32[]{:S(2)}, u32[]{:S(2)}) collective-permute-start(bf16[512,512]{1,0:T(8,128)(2,1)S(1)} %constant_dynamic-update-slice_fusion.refs_0_), channel_id=1, source_target_pairs={{0,32},{16,48},{32,0},{48,16},{1,33},{17,49},{33,1},{49,17},{2,34}... | collective-permute-start | bytes 1572872 | tf_op jit(solution)/shard_map/ppermute | solution.py:35
  192.3 24.5 %collective-permute-start.25 = (bf16[512,512]{1,0:T(8,128)(2,1)S(1)}, bf16[512,512]{1,0:T(8,128)(2,1)S(1)}, u32[]{:S(2)}, u32[]{:S(2)}) collective-permute-start(bf16[512,512]{1,0:T(8,128)(2,1)S(1)} %constant_dynamic-update-slice_fusion.refs_0_), channel_id=1, source_target_pairs={{0,48},{16,32},{32,16},{48,0},{1,49},{17,33},{33,17},{49,1},{2,50}... | collective-permute-start | bytes 1572872 | tf_op jit(solution)/shard_map/ppermute | solution.py:35
  193.3 25.8 %collective-permute-start.26 = (bf16[512,512]{1,0:T(8,128)(2,1)S(1)}, bf16[512,512]{1,0:T(8,128)(2,1)S(1)}, u32[]{:S(2)}, u32[]{:S(2)}) collective-permute-start(bf16[512,512]{1,0:T(8,128)(2,1)S(1)} %constant_dynamic-update-slice_fusion.refs_0_), channel_id=1, source_target_pairs={{0,8},{8,0},{1,9},{9,1},{2,10},{10,2},{3,11},{11,3},{4,12},{12,4},... | collective-permute-start | bytes 1572872 | tf_op jit(solution)/shard_map/ppermute | solution.py:35
  201.9 17.1 %collective-permute-start.27 = (bf16[512,512]{1,0:T(8,128)(2,1)S(1)}, bf16[512,512]{1,0:T(8,128)(2,1)S(1)}, u32[]{:S(2)}, u32[]{:S(2)}) collective-permute-start(bf16[512,512]{1,0:T(8,128)(2,1)S(1)} %collective-permute-done.23.refs_1_), channel_id=1, source_target_pairs={{0,8},{8,0},{1,9},{9,1},{2,10},{10,2},{3,11},{11,3},{4,12},{12,4},... | collective-permute-start | bytes 1572872 | tf_op jit(solution)/shard_map/ppermute | solution.py:35
  214.7 4.4 %collective-permute-start.28 = (bf16[512,512]{1,0:T(8,128)(2,1)S(1)}, bf16[512,512]{1,0:T(8,128)(2,1)S(1)}, u32[]{:S(2)}, u32[]{:S(2)}) collective-permute-start(bf16[512,512]{1,0:T(8,128)(2,1)S(1)} %collective-permute-done.24.refs_2_), channel_id=1, source_target_pairs={{0,8},{8,0},{1,9},{9,1},{2,10},{10,2},{3,11},{11,3},{4,12},{12,4},... | collective-permute-start | bytes 1572872 | tf_op jit(solution)/shard_map/ppermute | solution.py:35
  216.7 3.9 %collective-permute-start.29 = (bf16[512,512]{1,0:T(8,128)(2,1)S(1)}, bf16[512,512]{1,0:T(8,128)(2,1)S(1)}, u32[]{:S(2)}, u32[]{:S(2)}) collective-permute-start(bf16[512,512]{1,0:T(8,128)(2,1)S(1)} %collective-permute-done.25.refs_3_), channel_id=1, source_target_pairs={{0,8},{8,0},{1,9},{9,1},{2,10},{10,2},{3,11},{11,3},{4,12},{12,4},... | collective-permute-start | bytes 1572872 | tf_op jit(solution)/shard_map/ppermute | solution.py:35
Sparse Core Ops, SparseCore 0:
  10.4 58.3 all-gather.1
